TPU v7x, 256 devices: a whole 4x4x8 slice. The times are simulated.
256 devices in a mesh: blk: 8 (over y, x_hi), ulys: 32 (over z, x_lo, core).
Axes of the slice: x: 4 (x_hi: 2, x_lo: 2; x = x_hi * 2 + x_lo), y: 4, z: 8, core: 2. Of those that a mesh axis runs over, the one named last changes fastest.
Arguments:
- mamba_input: bfloat16 [16384, 16384], P(('blk', 'ulys')), may hold values from -6 to 6
- gate_input: bfloat16 [16384, 16384], P(('blk', 'ulys')), may hold values from -6 to 6
- delta_low: bfloat16 [16384, 512], P(('blk', 'ulys')), may hold values from -12 to 12
- state_mixers: bfloat16 [16384, 32], P(('blk', 'ulys')), may hold values from -6 to 6
- conv_weight: bfloat16 [4, 16384], P(None, 'ulys'), may hold values from -3 to 3
- conv_bias: float32 [16384], P('ulys'), may hold values from -3 to 3
- delta_weight: bfloat16 [512, 16384], P(None, 'ulys'), may hold values from -0.25 to 0.25
- delta_bias: float32 [16384], P('ulys'), may hold values from -12 to -2.3
- decay_log: float32 [16, 16384], P(None, 'ulys'), may hold values from -1 to 2.7
- skip_gain: float32 [16384], P('ulys'), may hold values from 0.5 to 1.5
- queries: bfloat16 [16384, 4096], P(('blk', 'ulys')), may hold values from -4.5 to 4.5
- key_rows: bfloat16 [16384, 1024], P(('blk', 'ulys')), may hold values from -4.5 to 4.5
- value_rows: bfloat16 [16384, 1024], P(('blk', 'ulys')), may hold values from -6 to 6
- span_order: int32 [16], replicated, may hold values from 0 to 15, as said below
Outputs:
- mamba_output: bfloat16 [16384, 16384], P(('blk', 'ulys'))
- attention_output: bfloat16 [16384, 4096], P(('blk', 'ulys'))
Inputs may be any that keep to these rules, and one draw needn't show every extreme that they name: `span_order`: device i of blk holds stored blocks 2i and 2i+1, whose sequence places are p and 15 - p for some p below 8, in either order; every sequence place appears once; the device holding places 0 and 15 and the device holding places 1 and 14 are 4 apart along blk.
All inputs are finite; a program needn't handle non-finite values.
Results may differ from a plain program's by a relative error of at most 0.013.
Values may be sent and summed in bfloat16 or wider, within the bound.
A program may use at most 128 MiB of HBM per device.

v0:
```python
import functools

import jax
import jax.numpy as jnp
from jax import lax
from jax.experimental import pallas as pl
from jax.experimental.pallas import tpu as pltpu
from jax.sharding import Mesh, PartitionSpec as P

STATE = 16
CONV = 4
HD = 128
SPAN = 1024
CHUNKS = 8
CLEN = 256
COLS = 512
TILES = COLS // 128
TB = 32
STEPS = CLEN // TB
NEG_LARGE = -1e30
LOG2E = 1.4426950408889634
VMEM_LIMIT = 56 * 2**20


def tree_sum(terms):
    while len(terms) > 1:
        terms = [a + b for a, b in zip(terms[::2], terms[1::2])] + terms[len(terms) // 2 * 2 :]
    return terms[0]


def scan_kernel(
    x_ref, prior_ref, low_ref, mix_ref, spread_ref, w_ref, convw_ref, convb_ref, bias_ref, rate_ref, skip_ref,
    y_ref, cum_ref, end_ref, sum_ref, total_ref,
    delta_s, dx_s, direct_s, splat_s, tail_s, state_s, run_s,
):
    step = pl.program_id(0)

    @pl.when(step == 0)
    def _():
        tail_s[...] = prior_ref[...]
        state_s[...] = jnp.zeros_like(state_s)
        run_s[...] = jnp.zeros_like(run_s)

    splat_s[...] = jnp.dot(mix_ref[...], spread_ref[...], preferred_element_type=jnp.float32)

    def prepare(chunk, carry):
        x = x_ref[chunk].astype(jnp.float32)
        padded = jnp.concatenate([tail_s[chunk], x], axis=0)
        mixed = convb_ref[...] + convw_ref[CONV - 1 : CONV, :] * x
        for k in range(CONV - 1):
            mixed = mixed + convw_ref[k : k + 1, :] * padded[8 - (CONV - 1) + k : 8 - (CONV - 1) + k + TB]
        tail_s[chunk] = x[TB - 8 :]
        driven = mixed * jax.nn.sigmoid(mixed)
        raw = jnp.dot(low_ref[chunk], w_ref[...], preferred_element_type=jnp.float32) + bias_ref[...]
        delta = jnp.maximum(raw, 0.0) + jnp.log1p(jnp.exp(-jnp.abs(raw)))
        dx = delta * driven
        direct = skip_ref[...] * driven
        for j in range(TILES):
            cols = slice(j * 128, (j + 1) * 128)
            rows = pl.ds(chunk, TB, stride=CHUNKS)
            delta_s.at[j][rows, :] = delta[:, cols]
            dx_s.at[j][rows, :] = dx[:, cols]
            direct_s.at[j][rows, :] = direct[:, cols]
        return carry

    lax.fori_loop(0, CHUNKS, prepare, 0)

    for j in range(TILES):
        cols = slice(j * 128, (j + 1) * 128)
        rates = [jnp.broadcast_to(rate_ref[n : n + 1, cols], (CHUNKS, 128)) for n in range(STATE)]

        def advance(t, carry):
            hidden, run = carry
            rows = pl.ds(pl.multiple_of(t * CHUNKS, CHUNKS), CHUNKS)
            delta = delta_s[j, rows, :]
            dx = dx_s[j, rows, :]
            hidden = tuple(
                jnp.exp2(delta * rates[n]) * hidden[n] + dx * splat_s[rows, n * 128 : (n + 1) * 128]
                for n in range(STATE)
            )
            terms = [
                hidden[n] * splat_s[rows, (STATE + n) * 128 : (STATE + n + 1) * 128] for n in range(STATE)
            ]
            run = run + delta
            y_ref[j, rows, :] = tree_sum(terms) + direct_s[j, rows, :]
            cum_ref[j, rows, :] = run
            return (hidden, run)

        hidden, run = lax.fori_loop(
            0, TB, advance, (tuple(state_s[j, n] for n in range(STATE)), run_s[j]), unroll=4
        )
        for n in range(STATE):
            state_s[j, n] = hidden[n]
        run_s[j] = run

    @pl.when(step == STEPS - 1)
    def _():
        for j in range(TILES):
            for n in range(STATE):
                end_ref.at[j][pl.ds(n, CHUNKS, stride=STATE), :] = state_s[j, n]
            sum_ref[j] = run_s[j]
        for j in range(TILES):
            rate = rate_ref[:, j * 128 : (j + 1) * 128]
            for b in range(2):
                state = jnp.zeros((STATE, 128), jnp.float32)
                total = jnp.zeros((1, 128), jnp.float32)
                for c in range(4 * b, 4 * b + 4):
                    here = sum_ref[j, c : c + 1, :]
                    state = jnp.exp2(rate * here) * state + end_ref[j, c * STATE : (c + 1) * STATE, :]
                    total = total + here
                total_ref[b, j, :STATE] = state
                total_ref[b, j, STATE:] = jnp.broadcast_to(total, (8, 128))


def scan_call(x, prior, low, mix, spread, w, convw, convb, bias, rate, skip):
    f32 = jnp.float32
    whole = lambda shape: pl.BlockSpec(shape, lambda i: (0,) * len(shape))
    tokens = lambda width: pl.BlockSpec((CHUNKS, TB, width), lambda i: (0, i, 0))
    rows = TB * CHUNKS
    return pl.pallas_call(
        scan_kernel,
        grid=(STEPS,),
        in_specs=[
            tokens(COLS), whole((CHUNKS, 8, COLS)), tokens(512),
            pl.BlockSpec((rows, 2 * STATE), lambda i: (i, 0)), whole((2 * STATE, 2 * STATE * 128)),
            whole((512, COLS)), whole((CONV, COLS)), whole((1, COLS)), whole((1, COLS)),
            whole((STATE, COLS)), whole((1, COLS)),
        ],
        out_specs=[
            pl.BlockSpec((TILES, rows, 128), lambda i: (0, i, 0)),
            pl.BlockSpec((TILES, rows, 128), lambda i: (0, i, 0)),
            whole((TILES, CHUNKS * STATE, 128)), whole((TILES, CHUNKS, 128)), whole((2, TILES, 24, 128)),
        ],
        out_shape=[
            jax.ShapeDtypeStruct((TILES, CLEN * CHUNKS, 128), f32),
            jax.ShapeDtypeStruct((TILES, CLEN * CHUNKS, 128), f32),
            jax.ShapeDtypeStruct((TILES, CHUNKS * STATE, 128), f32),
            jax.ShapeDtypeStruct((TILES, CHUNKS, 128), f32),
            jax.ShapeDtypeStruct((2, TILES, 24, 128), f32),
        ],
        scratch_shapes=[
            pltpu.VMEM((TILES, rows, 128), f32), pltpu.VMEM((TILES, rows, 128), f32),
            pltpu.VMEM((TILES, rows, 128), f32), pltpu.VMEM((rows, 2 * STATE * 128), f32),
            pltpu.VMEM((CHUNKS, 8, COLS), f32), pltpu.VMEM((TILES, STATE, CHUNKS, 128), f32),
            pltpu.VMEM((TILES, CHUNKS, 128), f32),
        ],
        compiler_params=pltpu.CompilerParams(vmem_limit_bytes=VMEM_LIMIT),
        cost_estimate=pl.CostEstimate(flops=100_000_000_000, bytes_accessed=16 * 2**20, transcendentals=0),
        name="scan_chunks",
    )(x, prior, low, mix, spread, w, convw, convb, bias, rate, skip)


def finish_kernel(
    info_ref, y_ref, cum_ref, mix_ref, spread_ref, gate_ref, rate_ref, end_ref, sum_ref, all_ref,
    out_ref, splat_s, start_s, enter_s, ready_s,
):
    step = pl.program_id(0)

    @pl.when(step == 0)
    def _():
        for j in range(TILES):
            rate = rate_ref[:, j * 128 : (j + 1) * 128]

            def carry_on(position, state):
                enter_s[position] = state
                block = info_ref[position]
                total = all_ref[block, j, STATE : STATE + 1, :]
                return jnp.exp2(rate * total) * state + all_ref[block, j, :STATE, :]

            lax.fori_loop(0, 2 * CHUNKS, carry_on, jnp.zeros((STATE, 128), jnp.float32))
            for b in range(2):
                state = enter_s[info_ref[2 * CHUNKS + b]]
                for c in range(4 * b, 4 * b + 4):
                    start_s[j, c * STATE : (c + 1) * STATE, :] = state
                    if c < 4 * b + 3:
                        state = (
                            jnp.exp2(rate * sum_ref[j, c : c + 1, :]) * state
                            + end_ref[j, c * STATE : (c + 1) * STATE, :]
                        )

    splat_s[...] = jnp.dot(mix_ref[...], spread_ref[...], preferred_element_type=jnp.float32)

    for j in range(TILES):
        cols = slice(j * 128, (j + 1) * 128)
        rates = [jnp.broadcast_to(rate_ref[n : n + 1, cols], (CHUNKS, 128)) for n in range(STATE)]
        starts = [start_s.at[j][pl.ds(n, CHUNKS, stride=STATE), :] for n in range(STATE)]

        def correct(t, carry):
            rows = pl.ds(pl.multiple_of(t * CHUNKS, CHUNKS), CHUNKS)
            run = cum_ref[j, rows, :]
            terms = [
                jnp.exp2(run * rates[n]) * starts[n] * splat_s[rows, n * 128 : (n + 1) * 128]
                for n in range(STATE)
            ]
            ready_s[j, rows, :] = tree_sum(terms) + y_ref[j, rows, :]
            return carry

        lax.fori_loop(0, TB, correct, 0, unroll=4)

    def gate_chunk(chunk, carry):
        for j in range(TILES):
            cols = slice(j * 128, (j + 1) * 128)
            ssm = ready_s.at[j][pl.ds(chunk, TB, stride=CHUNKS), :].astype(jnp.bfloat16).astype(jnp.float32)
            gate = gate_ref[chunk, :, cols].astype(jnp.float32)
            out_ref[chunk, :, cols] = (ssm * (gate * jax.nn.sigmoid(gate))).astype(jnp.bfloat16)
        return carry

    lax.fori_loop(0, CHUNKS, gate_chunk, 0)


def finish_call(info, y, cum, mix_out, spread, gate, rate, end, sums, every):
    f32 = jnp.float32
    whole = lambda shape: pl.BlockSpec(shape, lambda i, s: (0,) * len(shape))
    rows = TB * CHUNKS
    tiles = pl.BlockSpec((TILES, rows, 128), lambda i, s: (0, i, 0))
    return pl.pallas_call(
        finish_kernel,
        grid_spec=pltpu.PrefetchScalarGridSpec(
            num_scalar_prefetch=1,
            grid=(STEPS,),
            in_specs=[
                tiles, tiles, pl.BlockSpec((rows, STATE), lambda i, s: (i, 0)), whole((STATE, STATE * 128)),
                pl.BlockSpec((CHUNKS, TB, COLS), lambda i, s: (0, i, 0)),
                whole((STATE, COLS)), whole((TILES, CHUNKS * STATE, 128)), whole((TILES, CHUNKS, 128)),
                whole((2 * CHUNKS, TILES, 24, 128)),
            ],
            out_specs=pl.BlockSpec((CHUNKS, TB, COLS), lambda i, s: (0, i, 0)),
            scratch_shapes=[
                pltpu.VMEM((rows, STATE * 128), f32), pltpu.VMEM((TILES, CHUNKS * STATE, 128), f32),
                pltpu.VMEM((2 * CHUNKS, STATE, 128), f32), pltpu.VMEM((TILES, rows, 128), f32),
            ],
        ),
        out_shape=jax.ShapeDtypeStruct((CHUNKS, CLEN, COLS), jnp.bfloat16),
        compiler_params=pltpu.CompilerParams(vmem_limit_bytes=VMEM_LIMIT),
        cost_estimate=pl.CostEstimate(flops=50_000_000_000, bytes_accessed=16 * 2**20, transcendentals=0),
        name="finish_chunks",
    )(info, y, cum, mix_out, spread, gate, rate, end, sums, every)


QB = 256


def attention_kernel(side_ref, dev_ref, half_ref, diag_ref, first_ref, q_ref, kv_ref, o_ref, top_s, sum_s, acc_s):
    item = pl.program_id(0)
    scale = HD ** (-0.5) * LOG2E

    @pl.when(first_ref[item] == 1)
    def _():
        top_s[...] = jnp.full_like(top_s, NEG_LARGE)
        sum_s[...] = jnp.zeros_like(sum_s)
        acc_s[...] = jnp.zeros_like(acc_s)

    def absorb(masked):
        keys = kv_ref[0, :, 0, :, :HD].reshape(SPAN, HD)
        values = kv_ref[0, :, 0, :, HD:].reshape(SPAN, HD)
        for i in range(SPAN // QB):
            rows = slice(i * QB, (i + 1) * QB)
            scores = lax.dot_general(
                q_ref[0, rows, :], keys, (((1,), (1,)), ((), ())), preferred_element_type=jnp.float32
            ) * scale
            if masked:
                place = lax.broadcasted_iota(jnp.int32, (QB, SPAN), 1)
                key_pos = ((place // 64) % 4) * 256 + (place // 256) * 64 + place % 64
                query_pos = i * QB + lax.broadcasted_iota(jnp.int32, (QB, SPAN), 0)
                scores = jnp.where(key_pos <= query_pos, scores, NEG_LARGE)
            top = top_s[rows, :]
            new_top = jnp.maximum(top, jnp.max(scores, axis=1, keepdims=True))
            weights = jnp.exp2(scores - new_top[:, :1])
            shrink = jnp.exp2(top - new_top)
            top_s[rows, :] = new_top
            sum_s[rows, :] = sum_s[rows, :] * shrink + jnp.sum(weights, axis=1, keepdims=True)
            acc_s[rows, :] = acc_s[rows, :] * shrink + jnp.dot(
                weights.astype(jnp.bfloat16), values, preferred_element_type=jnp.float32
            )

    @pl.when(diag_ref[item] == 0)
    def _():
        absorb(False)

    @pl.when(diag_ref[item] == 1)
    def _():
        absorb(True)
        o_ref[0] = (acc_s[...] / sum_s[...]).astype(jnp.bfloat16)


def attention_call(side, dev, half, diag, first, q, kv):
    f32 = jnp.float32
    return pl.pallas_call(
        attention_kernel,
        grid_spec=pltpu.PrefetchScalarGridSpec(
            num_scalar_prefetch=5,
            grid=(17,),
            in_specs=[
                pl.BlockSpec((1, SPAN, HD), lambda i, side, dev, half, diag, first: (side[i], 0, 0)),
                pl.BlockSpec(
                    (1, 4, 1, 256, 2 * HD), lambda i, side, dev, half, diag, first: (dev[i], 0, half[i], 0, 0)
                ),
            ],
            out_specs=pl.BlockSpec((1, SPAN, HD), lambda i, side, dev, half, diag, first: (side[i], 0, 0)),
            scratch_shapes=[pltpu.VMEM((SPAN, 128), f32), pltpu.VMEM((SPAN, 128), f32), pltpu.VMEM((SPAN, HD), f32)],
        ),
        out_shape=jax.ShapeDtypeStruct((2, SPAN, HD), jnp.bfloat16),
        compiler_params=pltpu.CompilerParams(vmem_limit_bytes=VMEM_LIMIT),
        cost_estimate=pl.CostEstimate(flops=60_000_000_000, bytes_accessed=16 * 2**20, transcendentals=0),
        name="attend",
    )(side, dev, half, diag, first, q, kv)


ULYS = ("z", "w")
PLANE = ("blk", "w")


def small_gather(rows):
    return lax.all_gather(rows, "blk", axis=0, tiled=True)


def local(
    mamba_input, gate_input, delta_low, state_mixers, conv_weight, conv_bias, delta_weight, delta_bias,
    decay_log, skip_gain, queries, key_rows, value_rows, span_order,
):
    f32 = jnp.float32
    me = lax.axis_index("blk")
    places = jnp.arange(16, dtype=jnp.int32)
    holder = jnp.sum(jnp.where(span_order[None, :] == places[:, None], places[None, :], 0), axis=1)
    mine = lax.dynamic_slice_in_dim(span_order, 2 * me, 2, 0)

    x = lax.all_to_all(mamba_input, ULYS, split_axis=1, concat_axis=0, tiled=True)
    low_mix = lax.all_gather(
        jnp.concatenate([delta_low, state_mixers], axis=1), ULYS, axis=0, tiled=True
    )
    low = low_mix[:, :512].reshape(CHUNKS, CLEN, 512)
    mix = low_mix[:, 512:].reshape(CHUNKS, CLEN, 2 * STATE).swapaxes(0, 1).reshape(CHUNKS * CLEN, 2 * STATE)
    x = x.reshape(CHUNKS, CLEN, COLS)
    tails = small_gather(x[3::4, CLEN - 8 :, :])
    follows = (span_order[None, :] == mine[:, None] - 1).astype(jnp.bfloat16)
    before = jnp.einsum("cj,jtk->ctk", follows, tails, preferred_element_type=f32)
    ends = x[:, CLEN - 8 :, :].astype(f32)
    prior = jnp.concatenate([before[:1], ends[:3], before[1:], ends[4:7]], axis=0)
    spread = jnp.repeat(jnp.eye(2 * STATE, dtype=jnp.bfloat16), 128, axis=1)
    rate = -jnp.exp(decay_log) * LOG2E

    y, cum, end, sums, total = scan_call(
        x, prior, low, mix, spread, delta_weight, conv_weight.astype(f32), conv_bias[None, :],
        delta_bias[None, :], rate, skip_gain[None, :],
    )

    gate = lax.all_to_all(gate_input, ULYS, split_axis=1, concat_axis=0, tiled=True)
    query = lax.all_to_all(queries, ULYS, split_axis=1, concat_axis=0, tiled=True)
    kv = jnp.concatenate([key_rows.reshape(64, 8, HD), value_rows.reshape(64, 8, HD)], axis=2)
    kv = lax.all_to_all(kv.reshape(64, 8 * 2 * HD), "z", split_axis=1, concat_axis=0, tiled=True)
    kv = lax.all_gather(kv, PLANE, axis=0, tiled=True).reshape(8, 4, 2, 256, 2 * HD)

    items = jnp.arange(17, dtype=jnp.int32)
    second = (items > mine[0]).astype(jnp.int32)
    place = jnp.where(second == 1, items - mine[0] - 1, items)
    stored = jnp.sum(jnp.where(place[:, None] == span_order[None, :], places[None, :], 0), axis=1)
    diag = (place == jnp.where(second == 1, mine[1], mine[0])).astype(jnp.int32)
    first = (place == 0).astype(jnp.int32)
    attended = attention_call(
        second, stored // 2, stored % 2, diag, first, query.reshape(2, SPAN, HD), kv
    ).reshape(2 * SPAN, HD)

    every = small_gather(total)
    gated = finish_call(
        jnp.concatenate([holder, mine]), y, cum, mix[:, STATE:], spread[:STATE, : STATE * 128],
        gate.reshape(CHUNKS, CLEN, COLS), rate, end, sums, every,
    ).reshape(CHUNKS * CLEN, COLS)
    mamba_output = lax.all_to_all(gated, ULYS, split_axis=0, concat_axis=1, tiled=True)
    attention_output = lax.all_to_all(attended, ULYS, split_axis=0, concat_axis=1, tiled=True)
    return (mamba_output, attention_output)


def solution(mesh):
    tokens = P(("blk", "z", "w"), None)
    wide = P(None, ULYS)
    flat = P(ULYS)
    placed = (
        tokens, tokens, tokens, tokens, wide, flat, wide, flat, wide, flat, tokens, tokens, tokens, P(),
    )
    split_mesh = Mesh(mesh.devices.reshape(8, 8, 4), ("blk", "z", "w"))
    return jax.shard_map(
        local, mesh=split_mesh, in_specs=placed, out_specs=(tokens, tokens), check_vma=False
    )
```

profile of v0, /device:TPU:2, one launch (start us, length us, event | category | flops | bytes accessed | tf_op | source)
XLA Modules:
  0.0 356.3 jit_solution(11472043497122614490)
XLA Ops:
  7.2 0.9 copy.52
  8.2 1.5 pad_maximum_fusion.2
  9.7 0.9 copy.68
  10.6 0.9 copy.67
  11.6 0.8 copy.57
  12.3 8.5 %all-to-all-start.4 = ((bf16[64,8,256]{2,0,1:T(8,128)(2,1)}), bf16[64,8,256]{2,0,1:T(8,128)(2,1)S(1)}, u32[]{:S(2)}, u32[]{:S(2)}) async-start(bf16[64,8,256]{2,0,1:T(8,128)(2,1)} %copy.57), calls=%async_computation.4 | async-start | bytes 524288 | tf_op jit(solution)/shard_map/all_to_all | solution.py:350
  20.8 1.6 copy.78
  22.4 11.3 %all-to-all-done.4 = bf16[64,8,256]{2,0,1:T(8,128)(2,1)S(1)} async-done(((bf16[64,8,256]{2,0,1:T(8,128)(2,1)}), bf16[64,8,256]{2,0,1:T(8,128)(2,1)S(1)}, u32[]{:S(2)}, u32[]{:S(2)}) %all-to-all-start.4) | async-done | bytes 262176 | tf_op jit(solution)/shard_map/all_to_all | solution.py:350
  33.7 0.7 copy-done.4
  34.4 4.2 %all-to-all-start = ((bf16[64,32,512]{2,0,1:T(8,128)(2,1)}), bf16[64,32,512]{2,0,1:T(8,128)(2,1)S(1)}, u32[]{:S(2)}, u32[]{:S(2)}) async-start(bf16[64,32,512]{2,0,1:T(8,128)(2,1)} %bitcast.57), calls=%async_computation | async-start | bytes 4194304 | tf_op jit(solution)/shard_map/all_to_all | solution.py:327
  38.6 0.0 all-gather.5.cloned.1.call-start
  38.7 0.2 broadcast_in_dim.54
  38.9 0.1 copy.80
  39.0 0.7 convert_element_type.23.convw_ref
  39.7 0.6 slice.58.spread_ref
  40.3 3.2 copy.77
  43.6 0.1 broadcast_add_fusion
  43.6 0.6 fusion.9
  44.2 1.2 compare_convert_fusion.2.side_ref
  45.4 0.6 compare_select_fusion.4
  46.1 1.8 compare_convert_fusion
  47.9 0.1 select_reduce_fusion.1
  48.0 0.1 select_reduce_fusion
  48.1 0.7 pad_add_fusion.info_ref
  48.8 0.6 and_select_fusion
  49.3 0.6 negate_multiply_fusion.rate_ref
  50.0 1.0 copy_bitcast_fusion.3
  50.9 46.9 %all-to-all-done = bf16[64,32,512]{2,0,1:T(8,128)(2,1)S(1)} async-done(((bf16[64,32,512]{2,0,1:T(8,128)(2,1)}), bf16[64,32,512]{2,0,1:T(8,128)(2,1)S(1)}, u32[]{:S(2)}, u32[]{:S(2)}) %all-to-all-start) | async-done | bytes 2097184 | tf_op jit(solution)/shard_map/all_to_all | solution.py:327
  97.8 5.2 %all-to-all-start.1 = ((bf16[64,32,512]{2,0,1:T(8,128)(2,1)}), bf16[64,32,512]{2,0,1:T(8,128)(2,1)}, u32[]{:S(2)}, u32[]{:S(2)}) async-start(bf16[64,32,512]{2,0,1:T(8,128)(2,1)} %bitcast.56), calls=%async_computation.1 | async-start | bytes 4194304 | tf_op jit(solution)/shard_map/all_to_all | solution.py:347
  103.1 39.0 %all_gather.12 = bf16[16,8,512]{2,1,0:T(8,128)(2,1)S(1)} all-gather(bf16[2,8,512]{2,1,0:T(8,128)(2,1)S(1)} %slice.38), channel_id=1, replica_groups=mesh['blk'=8,'z'=8,'w'=4] {'blk'}, dimensions={0}, use_global_device_ids=true | all-gather | bytes 147456 | tf_op jit(solution)/shard_map/all_gather | solution.py:314
  142.0 0.2 fusion
  142.3 0.7 pad_maximum_fusion.1.prior_ref
  143.0 1.1 slice.56
  144.1 1.1 copy.79
  145.2 3.2 slice.55
  148.4 43.0 %scan_chunks.1 = (f32[4,2048,128]{2,1,0:T(8,128)}, f32[4,2048,128]{2,1,0:T(8,128)}, f32[4,128,128]{2,1,0:T(8,128)}, f32[4,8,128]{2,1,0:T(8,128)}, f32[2,4,24,128]{3,2,1,0:T(8,128)}) custom-call(bf16[8,256,512]{2,1,0:T(8,128)(2,1)} %bitcast.63, f32[8,8,512]{2,1,0:T(8,128)} %pad_maximum_fusion.1.prior_ref, bf16[8,256,512]{2,1,0:T(8,128)(2,1)} %bitcast.68, ...), custom_call_target="tpu_custom_call" | custom-call | flops 99999997952 | bytes 16777216 | tf_op jit(solution)/shard_map/scan_chunks/pallas_call | solution.py:120
  191.4 1.0 slice.57.mix_ref
  192.4 39.1 %all_gather.14.all_ref = f32[16,4,24,128]{3,2,1,0:T(8,128)} all-gather(f32[2,4,24,128]{3,2,1,0:T(8,128)} %get-tuple-element.11), channel_id=1, replica_groups=mesh['blk'=8,'z'=8,'w'=4] {'blk'}, dimensions={0}, use_global_device_ids=true | all-gather | bytes 884736 | tf_op jit(solution)/shard_map/all_gather | solution.py:314
  231.5 11.0 %all-to-all-start.3 = ((bf16[64,32,128]{2,0,1:T(8,128)(2,1)}), bf16[64,32,128]{2,0,1:T(8,128)(2,1)S(1)}, u32[]{:S(2)}, u32[]{:S(2)}) async-start(bf16[64,32,128]{2,0,1:T(8,128)(2,1)} %copy_bitcast_fusion.3), calls=%async_computation.3 | async-start | bytes 1048576 | tf_op jit(solution)/shard_map/all_to_all | solution.py:348
  242.5 24.4 %finish_chunks.1 = bf16[8,256,512]{2,1,0:T(8,128)(2,1)} custom-call(s32[18]{0:T(128)} %pad_add_fusion.info_ref, f32[4,2048,128]{2,1,0:T(8,128)} %get-tuple-element.7.y_ref, f32[4,2048,128]{2,1,0:T(8,128)} %get-tuple-element.8.cum_ref, bf16[2048,16]{1,0:T(8,128)(2,1)} %slice.57.mix_ref, bf16[16,2048]{1,0:T(8,128)(2,1)} %slice.58.spread_ref, ...), custom_call_target="tpu_custom_call" | custom-call | flops 49999998976 | bytes 16777216 | tf_op jit(solution)/shard_map/finish_chunks/pallas_call | solution.py:216
  266.9 0.8 copy-done.5
  267.7 8.3 %all-to-all-start.2 = ((bf16[32,64,512]{2,1,0:T(8,128)(2,1)}), bf16[32,64,512]{2,1,0:T(8,128)(2,1)S(1)}, u32[]{:S(2)}, u32[]{:S(2)}) async-start(bf16[32,64,512]{2,1,0:T(8,128)(2,1)} %bitcast.66), calls=%async_computation.2 | async-start | bytes 4194304 | tf_op jit(solution)/shard_map/all_to_all | solution.py:368
  276.0 46.5 %attend.1 = bf16[2,1024,128]{2,1,0:T(8,128)(2,1)} custom-call(s32[17]{0:T(128)} %compare_convert_fusion.2.side_ref, s32[17]{0:T(128)} %get-tuple-element.21.dev_ref, s32[17]{0:T(128)} %get-tuple-element.20.half_ref, s32[17]{0:T(128)} %get-tuple-element.23.diag_ref, s32[17]{0:T(128)} %get-tuple-element.22.first_ref, bf16[2,1024,128]{2,1,0:T(8,128)(2,1)} %bitcast.74, ...), custom_call_target="tpu_custom_call" | custom-call | flops 60000002048 | bytes 16777216 | tf_op jit(solution)/shard_map/attend/pallas_call | solution.py:288
  322.5 3.7 %all-to-all-done.2 = bf16[32,64,512]{2,1,0:T(8,128)(2,1)S(1)} async-done(((bf16[32,64,512]{2,1,0:T(8,128)(2,1)}), bf16[32,64,512]{2,1,0:T(8,128)(2,1)S(1)}, u32[]{:S(2)}, u32[]{:S(2)}) %all-to-all-start.2) | async-done | bytes 2097184 | tf_op jit(solution)/shard_map/all_to_all | solution.py:368
  326.2 4.7 %all-to-all-start.5 = ((bf16[32,64,128]{2,1,0:T(8,128)(2,1)}), bf16[32,64,128]{2,1,0:T(8,128)(2,1)S(1)}, u32[]{:S(2)}, u32[]{:S(2)}) async-start(bf16[32,64,128]{2,1,0:T(8,128)(2,1)} %bitcast.75), calls=%async_computation.5 | async-start | bytes 1048576 | tf_op jit(solution)/shard_map/all_to_all | solution.py:369
  330.9 1.5 copy.64
  332.4 16.2 %all-to-all-done.5 = bf16[32,64,128]{2,1,0:T(8,128)(2,1)S(1)} async-done(((bf16[32,64,128]{2,1,0:T(8,128)(2,1)}), bf16[32,64,128]{2,1,0:T(8,128)(2,1)S(1)}, u32[]{:S(2)}, u32[]{:S(2)}) %all-to-all-start.5) | async-done | bytes 524320 | tf_op jit(solution)/shard_map/all_to_all | solution.py:369
  348.6 0.9 copy_bitcast_fusion.2
  (33 shorter events, 0.2 us)
Async XLA Ops:
  7.2 42.8 %copy-start = (bf16[64,4096]{1,0:T(8,128)(2,1)S(1)}, bf16[64,4096]{1,0:T(8,128)(2,1)}, u32[]{:S(2)}) copy-start(bf16[64,4096]{1,0:T(8,128)(2,1)} %param.24) | copy-start | bytes 1572868
  7.2 13.6 %copy-start.2 = (bf16[64,16384]{1,0:T(8,128)(2,1)S(1)}, bf16[64,16384]{1,0:T(8,128)(2,1)}, u32[]{:S(2)}) copy-start(bf16[64,16384]{1,0:T(8,128)(2,1)} %param.14) | copy-start | bytes 6291460
  7.2 135.8 %all-gather.3.cloned.1.call-start = ((), (), s32[]{:S(2)}) async-start(), calls=%async_computation.6 | async-start | bytes 2703360 | tf_op jit(solution)/shard_map/all_gather | solution.py:328
  12.3 21.4 %all-to-all-start.4 = ((bf16[64,8,256]{2,0,1:T(8,128)(2,1)}), bf16[64,8,256]{2,0,1:T(8,128)(2,1)S(1)}, u32[]{:S(2)}, u32[]{:S(2)}) async-start(bf16[64,8,256]{2,0,1:T(8,128)(2,1)} %copy.57), calls=%async_computation.4 | async-start | bytes 524288 | tf_op jit(solution)/shard_map/all_to_all | solution.py:350
  33.7 0.7 copy-start.4
  33.7 5.3 %copy-start.8 = (bf16[4,512]{1,0:T(4,128)(2,1)S(1)}, bf16[4,512]{1,0:T(4,128)(2,1)}, u32[]{:S(2)}) copy-start(bf16[4,512]{1,0:T(4,128)(2,1)} %param.18) | copy-start | bytes 12292
  34.4 63.4 %all-to-all-start = ((bf16[64,32,512]{2,0,1:T(8,128)(2,1)}), bf16[64,32,512]{2,0,1:T(8,128)(2,1)S(1)}, u32[]{:S(2)}, u32[]{:S(2)}) async-start(bf16[64,32,512]{2,0,1:T(8,128)(2,1)} %bitcast.57), calls=%async_computation | async-start | bytes 4194304 | tf_op jit(solution)/shard_map/all_to_all | solution.py:327
  38.6 237.4 %all-gather.5.cloned.1.call-start = ((), (), s32[]{:S(2)}) async-start(), calls=%async_computation.7 | async-start | bytes 8650752 | tf_op jit(solution)/shard_map/all_gather | solution.py:351
  39.0 4.6 %copy-start.6 = (bf16[4,8,32,128]{3,1,2,0:T(8,128)(2,1)}, bf16[4,8,32,128]{3,1,2,0:T(8,128)(2,1)S(1)}, u32[]{:S(2)}) copy-start(bf16[4,8,32,128]{3,1,2,0:T(8,128)(2,1)S(1)} %copy.80) | copy-start | bytes 786436
  40.3 3.2 copy-start.9
  40.3 9.0 %copy-start.7 = (f32[16,512]{1,0:T(8,128)S(1)}, f32[16,512]{1,0:T(8,128)}, u32[]{:S(2)}) copy-start(f32[16,512]{1,0:T(8,128)} %param.22) | copy-start | bytes 98308
  97.8 44.5 %copy-start.1 = (bf16[64,32,512]{2,0,1:T(8,128)(2,1)}, bf16[64,32,512]{2,0,1:T(8,128)(2,1)S(1)}, u32[]{:S(2)}) copy-start(bf16[64,32,512]{2,0,1:T(8,128)(2,1)S(1)} %all-to-all-done) | copy-start | bytes 6291460
  97.8 133.7 %all-to-all-start.1 = ((bf16[64,32,512]{2,0,1:T(8,128)(2,1)}), bf16[64,32,512]{2,0,1:T(8,128)(2,1)}, u32[]{:S(2)}, u32[]{:S(2)}) async-start(bf16[64,32,512]{2,0,1:T(8,128)(2,1)} %bitcast.56), calls=%async_computation.1 | async-start | bytes 4194304 | tf_op jit(solution)/shard_map/all_to_all | solution.py:347
  148.4 43.0 %copy-start.3 = (bf16[8,256,32]{2,0,1:T(8,128)(2,1)S(1)}, bf16[8,256,32]{2,0,1:T(8,128)(2,1)}, u32[]{:S(2)}) copy-start(bf16[8,256,32]{2,0,1:T(8,128)(2,1)} %copy.79) | copy-start | bytes 393220
  231.5 35.4 %all-to-all-start.3 = ((bf16[64,32,128]{2,0,1:T(8,128)(2,1)}), bf16[64,32,128]{2,0,1:T(8,128)(2,1)S(1)}, u32[]{:S(2)}, u32[]{:S(2)}) async-start(bf16[64,32,128]{2,0,1:T(8,128)(2,1)} %copy_bitcast_fusion.3), calls=%async_computation.3 | async-start | bytes 1048576 | tf_op jit(solution)/shard_map/all_to_all | solution.py:348
  266.9 0.8 copy-start.5
  267.7 58.5 %all-to-all-start.2 = ((bf16[32,64,512]{2,1,0:T(8,128)(2,1)}), bf16[32,64,512]{2,1,0:T(8,128)(2,1)S(1)}, u32[]{:S(2)}, u32[]{:S(2)}) async-start(bf16[32,64,512]{2,1,0:T(8,128)(2,1)} %bitcast.66), calls=%async_computation.2 | async-start | bytes 4194304 | tf_op jit(solution)/shard_map/all_to_all | solution.py:368
  326.2 22.4 %all-to-all-start.5 = ((bf16[32,64,128]{2,1,0:T(8,128)(2,1)}), bf16[32,64,128]{2,1,0:T(8,128)(2,1)S(1)}, u32[]{:S(2)}, u32[]{:S(2)}) async-start(bf16[32,64,128]{2,1,0:T(8,128)(2,1)} %bitcast.75), calls=%async_computation.5 | async-start | bytes 1048576 | tf_op jit(solution)/shard_map/all_to_all | solution.py:369
Sparse Core Ops, SparseCore 0:
  9.9 83.3 all-gather.2
  95.8 66.7 all-gather.4
where the time goes:
time: 357 us; the launch traced here: 356 us
  Pallas kernels  114 us (32%)
  waiting for transfers between devices  78.2 us (22%)
  blocking collectives  78.1 us (22%)
  starting transfers between devices  42 us (12%)
  local copies, waits for them, and re-layouts  21.2 us (6%)
  between operations  14.3 us (4%)
  other arithmetic  8.62 us (2%)
    all_gather x2, blocking collectives, small_gather(): return lax.all_gather(rows, 'blk', axis=0, tiled=True)  78.1 us
    all_to_all x1, waiting for transfers between devices, local(): lax.all_to_all(mamba_input, ULYS, split_axis=1, concat_axis=0, tiled=True)  46.9 us
    pallas_call x1, Pallas kernels, attention_call(): pl.pallas_call(attention_kernel, grid_spec=pltpu.PrefetchScalarGridSpec(n...  46.5 us
    pallas_call x1, Pallas kernels, scan_call(): pl.pallas_call(scan_kernel, grid=(STEPS,), in_specs=[tokens(COLS), whole(...  43 us
    pallas_call x1, Pallas kernels, finish_call(): pl.pallas_call(finish_kernel, grid_spec=pltpu.PrefetchScalarGridSpec(num_...  24.4 us
    all_to_all x1, waiting for transfers between devices, local(): lax.all_to_all(attended, ULYS, split_axis=0, concat_axis=1, tiled=True)  16.2 us
    all_to_all x1, waiting for transfers between devices, local(): lax.all_to_all(kv.reshape(64, 8 * 2 * HD), 'z', split_axis=1, concat_axis...  11.3 us
    all_to_all x1, starting transfers between devices, local(): lax.all_to_all(queries, ULYS, split_axis=1, concat_axis=0, tiled=True)  11 us
  transfers between devices with their start and end apart: 8, of which 4 were waited for; matrix products, arithmetic and copies ran while one was open for 7% of the time, Pallas kernels for 32%

commit v1 on v0

--- a/solution.py
+++ b/solution.py
@@ -30,7 +30,7 @@
 
 def scan_kernel(
     x_ref, prior_ref, low_ref, mix_ref, spread_ref, w_ref, convw_ref, convb_ref, bias_ref, rate_ref, skip_ref,
-    y_ref, cum_ref, end_ref, sum_ref, total_ref,
+    y_ref, cum_ref, end_ref, sum_ref,
     delta_s, dx_s, direct_s, splat_s, tail_s, state_s, run_s,
 ):
     step = pl.program_id(0)
@@ -99,17 +99,6 @@
             for n in range(STATE):
                 end_ref.at[j][pl.ds(n, CHUNKS, stride=STATE), :] = state_s[j, n]
             sum_ref[j] = run_s[j]
-        for j in range(TILES):
-            rate = rate_ref[:, j * 128 : (j + 1) * 128]
-            for b in range(2):
-                state = jnp.zeros((STATE, 128), jnp.float32)
-                total = jnp.zeros((1, 128), jnp.float32)
-                for c in range(4 * b, 4 * b + 4):
-                    here = sum_ref[j, c : c + 1, :]
-                    state = jnp.exp2(rate * here) * state + end_ref[j, c * STATE : (c + 1) * STATE, :]
-                    total = total + here
-                total_ref[b, j, :STATE] = state
-                total_ref[b, j, STATE:] = jnp.broadcast_to(total, (8, 128))
 
 
 def scan_call(x, prior, low, mix, spread, w, convw, convb, bias, rate, skip):
@@ -129,14 +118,13 @@
         out_specs=[
             pl.BlockSpec((TILES, rows, 128), lambda i: (0, i, 0)),
             pl.BlockSpec((TILES, rows, 128), lambda i: (0, i, 0)),
-            whole((TILES, CHUNKS * STATE, 128)), whole((TILES, CHUNKS, 128)), whole((2, TILES, 24, 128)),
+            whole((TILES, CHUNKS * STATE, 128)), whole((TILES, CHUNKS, 128)),
         ],
         out_shape=[
             jax.ShapeDtypeStruct((TILES, CLEN * CHUNKS, 128), f32),
             jax.ShapeDtypeStruct((TILES, CLEN * CHUNKS, 128), f32),
             jax.ShapeDtypeStruct((TILES, CHUNKS * STATE, 128), f32),
             jax.ShapeDtypeStruct((TILES, CHUNKS, 128), f32),
-            jax.ShapeDtypeStruct((2, TILES, 24, 128), f32),
         ],
         scratch_shapes=[
             pltpu.VMEM((TILES, rows, 128), f32), pltpu.VMEM((TILES, rows, 128), f32),
@@ -150,40 +138,13 @@
     )(x, prior, low, mix, spread, w, convw, convb, bias, rate, skip)
 
 
-def finish_kernel(
-    info_ref, y_ref, cum_ref, mix_ref, spread_ref, gate_ref, rate_ref, end_ref, sum_ref, all_ref,
-    out_ref, splat_s, start_s, enter_s, ready_s,
-):
-    step = pl.program_id(0)
-
-    @pl.when(step == 0)
-    def _():
-        for j in range(TILES):
-            rate = rate_ref[:, j * 128 : (j + 1) * 128]
-
-            def carry_on(position, state):
-                enter_s[position] = state
-                block = info_ref[position]
-                total = all_ref[block, j, STATE : STATE + 1, :]
-                return jnp.exp2(rate * total) * state + all_ref[block, j, :STATE, :]
-
-            lax.fori_loop(0, 2 * CHUNKS, carry_on, jnp.zeros((STATE, 128), jnp.float32))
-            for b in range(2):
-                state = enter_s[info_ref[2 * CHUNKS + b]]
-                for c in range(4 * b, 4 * b + 4):
-                    start_s[j, c * STATE : (c + 1) * STATE, :] = state
-                    if c < 4 * b + 3:
-                        state = (
-                            jnp.exp2(rate * sum_ref[j, c : c + 1, :]) * state
-                            + end_ref[j, c * STATE : (c + 1) * STATE, :]
-                        )
-
+def finish_kernel(y_ref, cum_ref, mix_ref, spread_ref, gate_ref, rate_ref, start_ref, out_ref, splat_s, ready_s):
     splat_s[...] = jnp.dot(mix_ref[...], spread_ref[...], preferred_element_type=jnp.float32)
 
     for j in range(TILES):
         cols = slice(j * 128, (j + 1) * 128)
         rates = [jnp.broadcast_to(rate_ref[n : n + 1, cols], (CHUNKS, 128)) for n in range(STATE)]
-        starts = [start_s.at[j][pl.ds(n, CHUNKS, stride=STATE), :] for n in range(STATE)]
+        starts = [start_ref.at[j][pl.ds(n, CHUNKS, stride=STATE), :] for n in range(STATE)]
 
         def correct(t, carry):
             rows = pl.ds(pl.multiple_of(t * CHUNKS, CHUNKS), CHUNKS)
@@ -208,33 +169,26 @@
     lax.fori_loop(0, CHUNKS, gate_chunk, 0)
 
 
-def finish_call(info, y, cum, mix_out, spread, gate, rate, end, sums, every):
+def finish_call(y, cum, mix_out, spread, gate, rate, starts):
     f32 = jnp.float32
-    whole = lambda shape: pl.BlockSpec(shape, lambda i, s: (0,) * len(shape))
+    whole = lambda shape: pl.BlockSpec(shape, lambda i: (0,) * len(shape))
     rows = TB * CHUNKS
-    tiles = pl.BlockSpec((TILES, rows, 128), lambda i, s: (0, i, 0))
+    tiles = pl.BlockSpec((TILES, rows, 128), lambda i: (0, i, 0))
+    tokens = pl.BlockSpec((CHUNKS, TB, COLS), lambda i: (0, i, 0))
     return pl.pallas_call(
         finish_kernel,
-        grid_spec=pltpu.PrefetchScalarGridSpec(
-            num_scalar_prefetch=1,
-            grid=(STEPS,),
-            in_specs=[
-                tiles, tiles, pl.BlockSpec((rows, STATE), lambda i, s: (i, 0)), whole((STATE, STATE * 128)),
-                pl.BlockSpec((CHUNKS, TB, COLS), lambda i, s: (0, i, 0)),
-                whole((STATE, COLS)), whole((TILES, CHUNKS * STATE, 128)), whole((TILES, CHUNKS, 128)),
-                whole((2 * CHUNKS, TILES, 24, 128)),
-            ],
-            out_specs=pl.BlockSpec((CHUNKS, TB, COLS), lambda i, s: (0, i, 0)),
-            scratch_shapes=[
-                pltpu.VMEM((rows, STATE * 128), f32), pltpu.VMEM((TILES, CHUNKS * STATE, 128), f32),
-                pltpu.VMEM((2 * CHUNKS, STATE, 128), f32), pltpu.VMEM((TILES, rows, 128), f32),
-            ],
-        ),
+        grid=(STEPS,),
+        in_specs=[
+            tiles, tiles, pl.BlockSpec((rows, STATE), lambda i: (i, 0)), whole((STATE, STATE * 128)), tokens,
+            whole((STATE, COLS)), whole((TILES, CHUNKS * STATE, 128)),
+        ],
+        out_specs=tokens,
         out_shape=jax.ShapeDtypeStruct((CHUNKS, CLEN, COLS), jnp.bfloat16),
+        scratch_shapes=[pltpu.VMEM((rows, STATE * 128), f32), pltpu.VMEM((TILES, rows, 128), f32)],
         compiler_params=pltpu.CompilerParams(vmem_limit_bytes=VMEM_LIMIT),
         cost_estimate=pl.CostEstimate(flops=50_000_000_000, bytes_accessed=16 * 2**20, transcendentals=0),
         name="finish_chunks",
-    )(info, y, cum, mix_out, spread, gate, rate, end, sums, every)
+    )(y, cum, mix_out, spread, gate, rate, starts)
 
 
 QB = 256
@@ -306,12 +260,389 @@
     )(side, dev, half, diag, first, q, kv)
 
 
+WIDE = 640
+TAIL = 16
+MESH = pl.DeviceIdType.MESH
+
+
+def intake_kernel(
+    x_ref, low_ref, kv_ref, weight_ref, params_ref, x_out, low_out, tail_out, kv_out, weight_out, params_out, weight_mid, params_mid,
+    own_sem, kv_send, kv_recv, swap_send, swap_recv, x_send, x_recv, low_send, low_recv, col_send, col_recv, tail_send, tail_recv,
+):
+    blk, z, w = lax.axis_index("blk"), lax.axis_index("z"), lax.axis_index("w")
+    me = blk * 4 + w
+    barrier = pltpu.get_barrier_semaphore()
+
+    def greet(k, carry):
+        peer = lax.rem(me + k, 32)
+        pl.semaphore_signal(barrier, inc=1, device_id=(peer // 4, z, lax.rem(peer, 4)), device_id_type=MESH)
+        return carry
+
+    def greet_z(k, carry):
+        pl.semaphore_signal(barrier, inc=1, device_id=(blk, lax.rem(z + k, 8), w), device_id_type=MESH)
+        return carry
+
+    lax.fori_loop(1, 32, greet, 0)
+    lax.fori_loop(1, 8, greet_z, 0)
+
+    pl.semaphore_wait(barrier, 38)
+
+    def kv_copy(k):
+        peer = lax.rem(z + k, 8)
+        return pltpu.make_async_remote_copy(
+            src_ref=kv_ref.at[:, pl.ds(pl.multiple_of(peer * 2 * HD, 2 * HD), 2 * HD)], dst_ref=kv_out.at[z],
+            send_sem=kv_send.at[k], recv_sem=kv_recv.at[z], device_id=(blk, peer, w), device_id_type=MESH,
+        )
+
+    shift = lax.rem(blk - z + 8, 8)
+    held, middle, settled = (weight_ref, params_ref), (weight_mid, params_mid), (weight_out, params_out)
+
+    def along(slot):
+        return pltpu.make_async_remote_copy(
+            src_ref=held[slot], dst_ref=middle[slot], send_sem=swap_send.at[slot], recv_sem=swap_recv.at[slot],
+            device_id=(blk, shift, w), device_id_type=MESH,
+        )
+
+    def along_here(slot):
+        return pltpu.make_async_copy(held[slot], middle[slot], swap_recv.at[slot])
+
+    def across_plane(slot):
+        return pltpu.make_async_remote_copy(
+            src_ref=middle[slot], dst_ref=settled[slot], send_sem=swap_send.at[2 + slot],
+            recv_sem=swap_recv.at[2 + slot], device_id=(shift, z, w), device_id_type=MESH,
+        )
+
+    def across_here(slot):
+        return pltpu.make_async_copy(middle[slot], settled[slot], swap_recv.at[2 + slot])
+
+    def low_copy(k):
+        return pltpu.make_async_remote_copy(
+            src_ref=low_ref, dst_ref=low_out.at[blk, w], send_sem=low_send.at[k], recv_sem=low_recv.at[blk],
+            device_id=(lax.rem(blk + k, 8), z, w), device_id_type=MESH,
+        )
+
+    def x_copy(k):
+        peer = lax.rem(me + 1 + lax.rem(k - 1 + 11 * me, 31), 32)
+        return pltpu.make_async_remote_copy(
+            src_ref=x_ref.at[:, pl.ds(pl.multiple_of(peer * COLS, COLS), COLS)], dst_ref=x_out.at[blk, w],
+            send_sem=x_send.at[k], recv_sem=x_recv.at[me],
+            device_id=(peer // 4, z, lax.rem(peer, 4)), device_id_type=MESH,
+        )
+
+    def x_arrival(source):
+        return pltpu.make_async_remote_copy(
+            src_ref=x_out.at[source // 4, lax.rem(source, 4)], dst_ref=x_out.at[source // 4, lax.rem(source, 4)],
+            send_sem=x_send.at[0],
+            recv_sem=x_recv.at[source], device_id=(blk, z, w), device_id_type=MESH,
+        )
+
+    def start(copy):
+        def go(k, carry):
+            copy(k).start()
+            return carry
+
+        return go
+
+    own_low = pltpu.make_async_copy(low_ref, low_out.at[blk, w], own_sem.at[0])
+    own_x = pltpu.make_async_copy(
+        x_ref.at[:, pl.ds(pl.multiple_of(me * COLS, COLS), COLS)], x_out.at[blk, w], own_sem.at[1]
+    )
+    own_low.start()
+    lax.fori_loop(1, 8, start(low_copy), 0)
+    own_kv = pltpu.make_async_copy(
+        kv_ref.at[:, pl.ds(pl.multiple_of(z * 2 * HD, 2 * HD), 2 * HD)], kv_out.at[z], own_sem.at[2]
+    )
+
+    @pl.when(shift != z)
+    def _():
+        along(0).start()
+        along(1).start()
+
+    @pl.when(shift == z)
+    def _():
+        along_here(0).start()
+        along_here(1).start()
+
+    own_x.start()
+    own_kv.start()
+    lax.fori_loop(1, 12, start(x_copy), 0)
+    lax.fori_loop(1, 8, start(kv_copy), 0)
+
+    def low_arrived(k, carry):
+        source = lax.rem(blk + k, 8)
+        pltpu.make_async_remote_copy(
+            src_ref=low_out.at[source, w], dst_ref=low_out.at[source, w], send_sem=low_send.at[0],
+            recv_sem=low_recv.at[source], device_id=(blk, z, w), device_id_type=MESH,
+        ).wait_recv()
+        return carry
+
+    own_low.wait()
+    lax.fori_loop(1, 8, low_arrived, 0)
+    across = lax.rem(w + 2, 4)
+    sibling = (w // 2) * 2 + 1 - lax.rem(w, 2)
+    sibling_across = lax.rem(sibling + 2, 4)
+
+    def column(which, slot, target):
+        return pltpu.make_async_remote_copy(
+            src_ref=low_out.at[:, which], dst_ref=low_out.at[:, which], send_sem=col_send.at[slot],
+            recv_sem=col_recv.at[slot], device_id=(blk, z, target), device_id_type=MESH,
+        )
+
+    over = column(w, 0, across)
+    beside = column(w, 1, sibling)
+    over.start()
+    beside.start()
+    lax.fori_loop(12, 32, start(x_copy), 0)
+
+    @pl.when(shift != z)
+    def _():
+        for slot in range(2):
+            along(slot).wait_recv()
+            along(slot).wait_send()
+
+    @pl.when(shift == z)
+    def _():
+        along_here(0).wait()
+        along_here(1).wait()
+
+    @pl.when(z != 0)
+    def _():
+        across_plane(0).start()
+        across_plane(1).start()
+
+    @pl.when(z == 0)
+    def _():
+        across_here(0).start()
+        across_here(1).start()
+    column(across, 0, across).wait_recv()
+    relay = column(across, 2, sibling)
+    relay.start()
+
+    own_x.wait()
+
+    def wait_x(k, carry):
+        x_arrival(lax.rem(me + k, 32)).wait_recv()
+        return carry
+
+    lax.fori_loop(1, 32, wait_x, 0)
+
+    part, quarter = z // 4, lax.rem(z, 4)
+
+    def tail_copy(slot, which, target):
+        return pltpu.make_async_remote_copy(
+            src_ref=x_out.at[:, 3, pl.ds(64 - TAIL, TAIL)], dst_ref=tail_out.at[slot],
+            send_sem=tail_send.at[which], recv_sem=tail_recv.at[slot],
+            device_id=(blk, target, w), device_id_type=MESH,
+        )
+
+    @pl.when(quarter != 3)
+    def _():
+        tail_copy(0, 0, lax.rem(z + 1, 8)).start()
+
+    @pl.when(quarter == 3)
+    def _():
+        tail_copy(part, 0, 0).start()
+        tail_copy(part, 1, 4).start()
+
+    column(sibling, 1, sibling).wait_recv()
+    column(sibling_across, 2, sibling).wait_recv()
+
+    @pl.when(quarter != 0)
+    def _():
+        tail_copy(0, 0, lax.rem(z + 1, 8)).wait_recv()
+
+    @pl.when(quarter == 0)
+    def _():
+        tail_copy(0, 0, lax.rem(z + 1, 8)).wait_recv()
+        tail_copy(1, 0, lax.rem(z + 1, 8)).wait_recv()
+
+    tail_copy(0, 0, lax.rem(z + 1, 8)).wait_send()
+
+    @pl.when(quarter == 3)
+    def _():
+        tail_copy(0, 1, lax.rem(z + 1, 8)).wait_send()
+
+    def low_sent(k, carry):
+        low_copy(k).wait_send()
+        return carry
+
+    def x_sent(k, carry):
+        x_copy(k).wait_send()
+        return carry
+
+    own_kv.wait()
+
+    def kv_done(k, carry):
+        source = lax.rem(z + k, 8)
+        pltpu.make_async_remote_copy(
+            src_ref=kv_out.at[source], dst_ref=kv_out.at[source], send_sem=kv_send.at[0],
+            recv_sem=kv_recv.at[source], device_id=(blk, z, w), device_id_type=MESH,
+        ).wait_recv()
+        kv_copy(k).wait_send()
+        return carry
+
+    lax.fori_loop(1, 8, kv_done, 0)
+
+    @pl.when(z != 0)
+    def _():
+        for slot in range(2):
+            across_plane(slot).wait_recv()
+            across_plane(slot).wait_send()
+
+    @pl.when(z == 0)
+    def _():
+        across_here(0).wait()
+        across_here(1).wait()
+
+    lax.fori_loop(1, 8, low_sent, 0)
+    lax.fori_loop(1, 32, x_sent, 0)
+    over.wait_send()
+    beside.wait_send()
+    relay.wait_send()
+
+
+def intake_call(x, low, kv, weight, params):
+    anywhere = pl.BlockSpec(memory_space=pl.ANY)
+    sems = pltpu.SemaphoreType.DMA
+    return pl.pallas_call(
+        intake_kernel,
+        in_specs=[anywhere] * 5,
+        out_specs=[anywhere] * 8,
+        out_shape=[
+            jax.ShapeDtypeStruct((8, 4, 64, COLS), jnp.bfloat16),
+            jax.ShapeDtypeStruct((8, 4, 64, WIDE), jnp.bfloat16),
+            jax.ShapeDtypeStruct((2, 8, TAIL, COLS), jnp.bfloat16),
+            jax.ShapeDtypeStruct((8, 64, 2 * HD), jnp.bfloat16),
+            jax.ShapeDtypeStruct(weight.shape, weight.dtype),
+            jax.ShapeDtypeStruct(params.shape, params.dtype),
+            jax.ShapeDtypeStruct(weight.shape, weight.dtype),
+            jax.ShapeDtypeStruct(params.shape, params.dtype),
+        ],
+        scratch_shapes=[
+            sems((3,)), sems((8,)), sems((8,)), sems((4,)), sems((4,)), sems((32,)), sems((32,)), sems((8,)), sems((8,)),
+            sems((3,)), sems((3,)),
+            sems((2,)), sems((2,)),
+        ],
+        compiler_params=pltpu.CompilerParams(collective_id=0, has_side_effects=True),
+        name="intake",
+    )(x, low, kv, weight, params)
+
+
+def states_kernel(
+    order_ref, end_ref, sum_ref, rate_ref, start_ref,
+    got_end, got_sum, chain, reply, own_sem, end_send, end_recv, sum_send, sum_recv, back_send, back_recv,
+):
+    blk, z, w = lax.axis_index("blk"), lax.axis_index("z"), lax.axis_index("w")
+    barrier = pltpu.get_barrier_semaphore()
+
+    def greet(k, carry):
+        pl.semaphore_signal(barrier, inc=1, device_id=(blk, lax.rem(z + k, 8), w), device_id_type=MESH)
+        return carry
+
+    lax.fori_loop(1, 8, greet, 0)
+    pl.semaphore_wait(barrier, 7)
+    mine = pl.ds(pl.multiple_of(z * 8, 8), 8)
+
+    def remote(src, dst, send, recv, target):
+        return pltpu.make_async_remote_copy(
+            src_ref=src, dst_ref=dst, send_sem=send, recv_sem=recv, device_id=(blk, target, w), device_id_type=MESH
+        )
+
+    def end_copy(k):
+        peer = lax.rem(z + k, 8)
+        return remote(
+            end_ref.at[peer // 2, :, lax.rem(peer, 2)], got_end.at[mine], end_send.at[k], end_recv.at[z], peer
+        )
+
+    def sum_copy(k):
+        peer = lax.rem(z + k, 8)
+        return remote(sum_ref.at[peer // 2], got_sum.at[mine], sum_send.at[k], sum_recv.at[z], peer)
+
+    def back_copy(k):
+        peer = lax.rem(z + k, 8)
+        return remote(
+            reply.at[pl.ds(pl.multiple_of(peer * 8, 8), 8)], start_ref.at[z // 2, :, lax.rem(z, 2)],
+            back_send.at[k], back_recv.at[z], peer,
+        )
+
+    def send_ends(k, carry):
+        end_copy(k).start()
+        sum_copy(k).start()
+        return carry
+
+    lax.fori_loop(1, 8, send_ends, 0)
+    own_end = pltpu.make_async_copy(end_ref.at[z // 2, :, lax.rem(z, 2)], got_end.at[mine], own_sem.at[0])
+    own_sum = pltpu.make_async_copy(sum_ref.at[z // 2], got_sum.at[mine], own_sem.at[1])
+    own_end.start()
+    own_sum.start()
+    own_end.wait()
+    own_sum.wait()
+
+    def ends_arrived(k, carry):
+        source = lax.rem(z + k, 8)
+        there = pl.ds(pl.multiple_of(source * 8, 8), 8)
+        remote(got_end.at[there], got_end.at[there], end_send.at[0], end_recv.at[source], z).wait_recv()
+        remote(got_sum.at[there], got_sum.at[there], sum_send.at[0], sum_recv.at[source], z).wait_recv()
+        return carry
+
+    lax.fori_loop(1, 8, ends_arrived, 0)
+    rate = rate_ref[z // 2, lax.rem(z, 2)]
+
+    def carry_on(position, state):
+        chain[position] = state
+        index = order_ref[position]
+        return jnp.exp2(rate * got_sum[pl.ds(index, 1), :]) * state + got_end[index]
+
+    lax.fori_loop(0, 64, carry_on, jnp.zeros((8, 128), jnp.float32))
+
+    def pick(index, carry):
+        reply[index] = chain[order_ref[64 + index]]
+        return carry
+
+    lax.fori_loop(0, 64, pick, 0)
+
+    def send_back(k, carry):
+        back_copy(k).start()
+        return carry
+
+    lax.fori_loop(1, 8, send_back, 0)
+    own_back = pltpu.make_async_copy(reply.at[mine], start_ref.at[z // 2, :, lax.rem(z, 2)], own_sem.at[2])
+    own_back.start()
+    own_back.wait()
+
+    def finish(k, carry):
+        source = lax.rem(z + k, 8)
+        landed = start_ref.at[source // 2, :, lax.rem(source, 2)]
+        remote(landed, landed, back_send.at[0], back_recv.at[source], z).wait_recv()
+        end_copy(k).wait_send()
+        sum_copy(k).wait_send()
+        back_copy(k).wait_send()
+        return carry
+
+    lax.fori_loop(1, 8, finish, 0)
+
+
+def states_call(order, ends, sums, rate):
+    f32 = jnp.float32
+    here = pl.BlockSpec(memory_space=pltpu.VMEM)
+    sems = pltpu.SemaphoreType.DMA
+    return pl.pallas_call(
+        states_kernel,
+        in_specs=[pl.BlockSpec(memory_space=pltpu.SMEM), here, here, here],
+        out_specs=here,
+        out_shape=jax.ShapeDtypeStruct((TILES, CHUNKS, 2, 8, 128), f32),
+        scratch_shapes=[
+            pltpu.VMEM((64, 8, 128), f32), pltpu.VMEM((64, 128), f32), pltpu.VMEM((64, 8, 128), f32),
+            pltpu.VMEM((64, 8, 128), f32), sems((3,)), sems((8,)), sems((8,)), sems((8,)), sems((8,)),
+            sems((8,)), sems((8,)),
+        ],
+        compiler_params=pltpu.CompilerParams(collective_id=1, has_side_effects=True),
+        name="chain_states",
+    )(order, ends, sums, rate)
+
+
 ULYS = ("z", "w")
 PLANE = ("blk", "w")
-
-
-def small_gather(rows):
-    return lax.all_gather(rows, "blk", axis=0, tiled=True)
 
 
 def local(
@@ -319,53 +650,75 @@
     decay_log, skip_gain, queries, key_rows, value_rows, span_order,
 ):
     f32 = jnp.float32
-    me = lax.axis_index("blk")
+    me, z = lax.axis_index("blk"), lax.axis_index("z")
+    zpart = z // 4
+    params = jnp.concatenate(
+        [
+            -jnp.exp(decay_log) * LOG2E, conv_weight.astype(f32), conv_bias[None, :], delta_bias[None, :],
+            skip_gain[None, :], jnp.zeros((1, COLS), f32),
+        ],
+        axis=0,
+    )
     places = jnp.arange(16, dtype=jnp.int32)
-    holder = jnp.sum(jnp.where(span_order[None, :] == places[:, None], places[None, :], 0), axis=1)
     mine = lax.dynamic_slice_in_dim(span_order, 2 * me, 2, 0)
 
-    x = lax.all_to_all(mamba_input, ULYS, split_axis=1, concat_axis=0, tiled=True)
-    low_mix = lax.all_gather(
-        jnp.concatenate([delta_low, state_mixers], axis=1), ULYS, axis=0, tiled=True
-    )
-    low = low_mix[:, :512].reshape(CHUNKS, CLEN, 512)
-    mix = low_mix[:, 512:].reshape(CHUNKS, CLEN, 2 * STATE).swapaxes(0, 1).reshape(CHUNKS * CLEN, 2 * STATE)
+    low_mix = jnp.concatenate(
+        [delta_low, state_mixers, jnp.zeros((64, WIDE - 512 - 2 * STATE), jnp.bfloat16)], axis=1
+    )
+    kv = jnp.concatenate([key_rows.reshape(64, 8, HD), value_rows.reshape(64, 8, HD)], axis=2)
+    x, low_mix, tails, kv, weight, params, _, _ = intake_call(
+        mamba_input, low_mix, kv.reshape(64, 8 * 2 * HD), delta_weight, params
+    )
+    x, gate_input, queries = lax.optimization_barrier((x, gate_input, queries))
+    rate = params[:STATE]
+    low = low_mix.reshape(CHUNKS, CLEN, WIDE)
+    mix = (
+        low[:, :, 512 : 512 + 2 * STATE].swapaxes(0, 1).reshape(CHUNKS * CLEN, 2 * STATE)
+    )
     x = x.reshape(CHUNKS, CLEN, COLS)
-    tails = small_gather(x[3::4, CLEN - 8 :, :])
-    follows = (span_order[None, :] == mine[:, None] - 1).astype(jnp.bfloat16)
-    before = jnp.einsum("cj,jtk->ctk", follows, tails, preferred_element_type=f32)
-    ends = x[:, CLEN - 8 :, :].astype(f32)
-    prior = jnp.concatenate([before[:1], ends[:3], before[1:], ends[4:7]], axis=0)
+    places = places[:, None]
+    earlier = span_order.reshape(CHUNKS, 2)[:, zpart] - 1
+    follows = (earlier[:, None] == span_order[None, :]).astype(jnp.bfloat16)
+    at_start = lax.rem(z, 4) == 0
+    tails = tails[:, :, TAIL - 8 :]
+    of_block = tails.swapaxes(0, 1).reshape(16, 8, COLS)
+    before = jnp.einsum("cj,jtk->ctk", follows, of_block, preferred_element_type=f32)
+    prior = jnp.where(at_start, before, tails[0].astype(f32))
     spread = jnp.repeat(jnp.eye(2 * STATE, dtype=jnp.bfloat16), 128, axis=1)
-    rate = -jnp.exp(decay_log) * LOG2E
-
-    y, cum, end, sums, total = scan_call(
-        x, prior, low, mix, spread, delta_weight, conv_weight.astype(f32), conv_bias[None, :],
-        delta_bias[None, :], rate, skip_gain[None, :],
-    )
-
-    gate = lax.all_to_all(gate_input, ULYS, split_axis=1, concat_axis=0, tiled=True)
+
+    y, cum, end, sums = scan_call(
+        x, prior, low, mix, spread, weight, params[16:20], params[20:21], params[21:22], rate, params[22:23],
+    )
+
+    gate = lax.all_to_all(gate_input, PLANE, split_axis=1, concat_axis=0, tiled=True)
     query = lax.all_to_all(queries, ULYS, split_axis=1, concat_axis=0, tiled=True)
-    kv = jnp.concatenate([key_rows.reshape(64, 8, HD), value_rows.reshape(64, 8, HD)], axis=2)
-    kv = lax.all_to_all(kv.reshape(64, 8 * 2 * HD), "z", split_axis=1, concat_axis=0, tiled=True)
-    kv = lax.all_gather(kv, PLANE, axis=0, tiled=True).reshape(8, 4, 2, 256, 2 * HD)
+    kv = lax.all_gather(kv.reshape(512, 2 * HD), PLANE, axis=0, tiled=True).reshape(8, 4, 2, 256, 2 * HD)
 
     items = jnp.arange(17, dtype=jnp.int32)
     second = (items > mine[0]).astype(jnp.int32)
     place = jnp.where(second == 1, items - mine[0] - 1, items)
-    stored = jnp.sum(jnp.where(place[:, None] == span_order[None, :], places[None, :], 0), axis=1)
+    stored = jnp.sum(jnp.where(place[:, None] == span_order[None, :], places.T, 0), axis=1)
     diag = (place == jnp.where(second == 1, mine[1], mine[0])).astype(jnp.int32)
     first = (place == 0).astype(jnp.int32)
     attended = attention_call(
         second, stored // 2, stored % 2, diag, first, query.reshape(2, SPAN, HD), kv
     ).reshape(2 * SPAN, HD)
 
-    every = small_gather(total)
+    steps = jnp.arange(64, dtype=jnp.int32)
+    at = jnp.sum(jnp.where((steps // 4)[:, None] == span_order[None, :], places.T, 0), axis=1)
+    index_of = ((at % 2) * 4 + steps % 4) * 8 + at // 2
+    block_of = 2 * (steps % 8) + steps // 32
+    place_of = jnp.sum(jnp.where(block_of[:, None] == places.T, span_order[None, :], 0), axis=1)
+    position_of = place_of * 4 + (steps // 8) % 4
+    starts = states_call(
+        jnp.concatenate([index_of, position_of]), end.reshape(TILES, CHUNKS, 2, 8, 128), sums,
+        rate.reshape(2, 8, TILES, 128).transpose(2, 0, 1, 3),
+    )
     gated = finish_call(
-        jnp.concatenate([holder, mine]), y, cum, mix[:, STATE:], spread[:STATE, : STATE * 128],
-        gate.reshape(CHUNKS, CLEN, COLS), rate, end, sums, every,
+        y, cum, mix[:, STATE:], spread[:STATE, : STATE * 128], gate.reshape(CHUNKS, CLEN, COLS), rate,
+        starts.reshape(TILES, CHUNKS * STATE, 128),
     ).reshape(CHUNKS * CLEN, COLS)
-    mamba_output = lax.all_to_all(gated, ULYS, split_axis=0, concat_axis=1, tiled=True)
+    mamba_output = lax.all_to_all(gated, PLANE, split_axis=0, concat_axis=1, tiled=True)
     attention_output = lax.all_to_all(attended, ULYS, split_axis=0, concat_axis=1, tiled=True)
     return (mamba_output, attention_output)
 

time: 357 us -> 293 us (0.82)
  Pallas kernels: 114 us -> 202 us
  blocking collectives: 78.1 us -> 0 us
  waiting for transfers between devices: 78.2 us -> 16.9 us
  starting transfers between devices: 42 us -> 28.8 us
    pallas_call x1 -> x3, Pallas kernels: 24.4 us -> 113 us  [the longest x1 62.5 us: intake_call(): pl.pallas_call(intake_kernel, in_specs=[anywhere] * 5, out_specs=[anywher...]
    all_gather x2 -> x0, blocking collectives: 78.1 us -> none  [small_gather(): return lax.all_gather(rows, 'blk', axis=0, tiled=True)]
    all_to_all x4 -> x2, waiting for transfers between devices: 61.9 us -> 0.01 us  [the longest x1 0.01 us: local(): lax.all_to_all(gate_input, PLANE, split_axis=1, concat_axis=0, tiled=True)]
    all_to_all x4 -> x2, starting transfers between devices: 26.2 us -> 16 us  [the longest x1 8.76 us: local(): lax.all_to_all(gate_input, PLANE, split_axis=1, concat_axis=0, tiled=True)]
    all_to_all x1, starting transfers between devices: 11 us -> 4.33 us  [local(): lax.all_to_all(queries, ULYS, split_axis=1, concat_axis=0, tiled=True)]
    all_to_all x1, starting transfers between devices: 4.67 us -> 8.37 us  [local(): lax.all_to_all(attended, ULYS, split_axis=0, concat_axis=1, tiled=True)]
  transfers between devices with their start and end apart: 8 -> 5, of which waited for: 4 -> 1; matrix products, arithmetic and copies ran while one was open for 7% -> 6% of each run, Pallas kernels for 32% -> 48%
where the time goes in v1:
time: 293 us; the launch traced here: 292 us
  Pallas kernels  202 us (69%)
  starting transfers between devices  28.8 us (10%)
  local copies, waits for them, and re-layouts  20.1 us (7%)
  waiting for transfers between devices  16.9 us (6%)
  between operations  14.2 us (5%)
  other arithmetic  9.13 us (3%)
    pallas_call x1, Pallas kernels, intake_call(): pl.pallas_call(intake_kernel, in_specs=[anywhere] * 5, out_specs=[anywher...  62.5 us
    pallas_call x1, Pallas kernels, attention_call(): pl.pallas_call(attention_kernel, grid_spec=pltpu.PrefetchScalarGridSpec(n...  46.5 us
    pallas_call x1, Pallas kernels, scan_call(): pl.pallas_call(scan_kernel, grid=(STEPS,), in_specs=[tokens(COLS), whole(...  42.8 us
    pallas_call x1, Pallas kernels, states_call(): pl.pallas_call(states_kernel, in_specs=[pl.BlockSpec(memory_space=pltpu.S...  27.9 us
    pallas_call x1, Pallas kernels, finish_call(): pl.pallas_call(finish_kernel, grid=(STEPS,), in_specs=[tiles, tiles, pl.B...  22.6 us
    all_to_all x1, waiting for transfers between devices, local(): lax.all_to_all(attended, ULYS, split_axis=0, concat_axis=1, tiled=True)  16.2 us
    all_to_all x1, starting transfers between devices, local(): lax.all_to_all(gate_input, PLANE, split_axis=1, concat_axis=0, tiled=True)  8.76 us
    all_to_all x1, starting transfers between devices, local(): lax.all_to_all(attended, ULYS, split_axis=0, concat_axis=1, tiled=True)  8.37 us
  transfers between devices with their start and end apart: 5, of which 1 were waited for; matrix products, arithmetic and copies ran while one was open for 6% of the time, Pallas kernels for 48%

profile of v1, /device:TPU:2, one launch (start us, length us, event | category | flops | bytes accessed | tf_op | source)
XLA Modules:
  0.0 291.7 jit_solution(13583642100455741801)
XLA Ops:
  7.2 1.0 copy.48
  8.2 0.9 copy.49
  9.1 0.8 copy.50
  9.9 0.8 copy.34
  10.7 0.8 negate_multiply_fusion
  11.5 0.1 pad.6.clone
  11.6 1.5 maximum_maximum_fusion.low_ref
  13.1 2.0 concatenate.14.params_ref
  15.0 62.5 %intake.1 = (bf16[8,4,64,512]{3,2,1,0:T(8,128)(2,1)}, bf16[8,4,64,640]{3,2,1,0:T(8,128)(2,1)}, bf16[2,8,16,512]{3,2,1,0:T(8,128)(2,1)}, bf16[8,64,256]{2,1,0:T(8...) custom-call(bf16[64,16384]{1,0:T(8,128)(2,1)} %x_ref.1, ...), custom_call_target="tpu_custom_call" | custom-call | tf_op jit(solution)/shard_map/intake/pallas_call | solution.py:507
  77.5 1.6 copy.61
  79.1 8.8 %all-to-all-start = ((bf16[64,32,512]{2,0,1:T(8,128)(2,1)}), bf16[64,32,512]{2,0,1:T(8,128)(2,1)S(1)}, u32[]{:S(2)}, u32[]{:S(2)}) async-start(bf16[64,32,512]{2,0,1:T(8,128)(2,1)} %bitcast.62), calls=%async_computation | async-start | bytes 4194304 | tf_op jit(solution)/shard_map/all_to_all | solution.py:693
  87.9 0.0 all-gather.2.cloned.1.call-start
  87.9 0.7 all-gather.2.cloned.1.call-update
  88.6 0.6 slice_bitcast_fusion.2
  89.2 0.6 fusion.16
  89.8 1.1 slice_bitcast_fusion
  90.9 0.6 slice.42.convw_ref
  91.5 0.1 reshape.123
  91.6 1.1 copy.62
  92.8 0.2 broadcast_in_dim.69
  93.0 0.8 copy.63
  93.8 0.2 add_reduce_fusion
  94.0 0.2 fusion
  94.2 1.6 convert_select_fusion.prior_ref
  95.8 42.8 %scan_chunks.1 = (f32[4,2048,128]{2,1,0:T(8,128)}, f32[4,2048,128]{2,1,0:T(8,128)}, f32[4,128,128]{2,1,0:T(8,128)}, f32[4,8,128]{2,1,0:T(8,128)}) custom-call(bf16[8,256,512]{2,1,0:T(8,128)(2,1)} %bitcast.95, f32[8,8,512]{2,1,0:T(8,128)} %convert_select_fusion.prior_ref, bf16[8,256,640]{2,1,0:T(8,128)(2,1)} %bitcast.90, bf16[2048,32]{1,0:T(8,128)(2,1)} %bitcast.71, ...), custom_call_target="tpu_custom_call" | custom-call | flops 99999997952 | bytes 16777216 | tf_op jit(solution)/shard_map/scan_chunks/pallas_call | solution.py:109
  138.6 1.0 slice.52.mix_ref
  139.6 1.5 slice.53.spread_ref
  141.1 0.6 copy.64
  141.7 0.1 dynamic_slice.7
  141.8 0.1 select_reduce_fusion.2
  141.9 0.6 pad_add_fusion.order_ref
  142.5 27.9 %chain_states.1 = f32[4,8,2,8,128]{4,3,2,1,0:T(8,128)} custom-call(s32[128]{0:T(128)} %pad_add_fusion.order_ref, f32[4,8,2,8,128]{4,3,2,1,0:T(8,128)} %bitcast.84, f32[4,8,128]{2,1,0:T(8,128)} %get-tuple-element.25.sum_ref, f32[4,2,8,128]{3,2,1,0:T(8,128)} %bitcast.88), custom_call_target="tpu_custom_call" | custom-call | tf_op jit(solution)/shard_map/chain_states/pallas_call | solution.py:629
  170.4 0.6 fusion.17
  171.0 0.6 compare_select_fusion.9
  171.6 1.2 compare_convert_fusion.2.side_ref
  172.9 1.8 compare_convert_fusion
  174.7 0.1 select_reduce_fusion
  174.8 0.6 and_select_fusion
  175.4 1.0 copy_bitcast_fusion.2
  176.3 4.3 %all-to-all-start.2 = ((bf16[64,32,128]{2,0,1:T(8,128)(2,1)}), bf16[64,32,128]{2,0,1:T(8,128)(2,1)S(1)}, u32[]{:S(2)}, u32[]{:S(2)}) async-start(bf16[64,32,128]{2,0,1:T(8,128)(2,1)} %copy_bitcast_fusion.2), calls=%async_computation.2 | async-start | bytes 1048576 | tf_op jit(solution)/shard_map/all_to_all | solution.py:694
  180.7 22.6 %finish_chunks.1 = bf16[8,256,512]{2,1,0:T(8,128)(2,1)} custom-call(f32[4,2048,128]{2,1,0:T(8,128)} %get-tuple-element.21.y_ref, f32[4,2048,128]{2,1,0:T(8,128)} %get-tuple-element.22.cum_ref, bf16[2048,16]{1,0:T(8,128)(2,1)} %slice.52.mix_ref, bf16[16,2048]{1,0:T(8,128)(2,1)} %slice.53.spread_ref, bf16[8,256,512]{2,1,0:T(8,128)(2,1)} %bitcast.68, ...), custom_call_target="tpu_custom_call" | custom-call | flops 49999998976 | bytes 16777216 | tf_op jit(solution)/shard_map/finish_chunks/pallas_call | solution.py:178
  203.3 0.8 copy-done.4
  204.1 7.3 %all-to-all-start.1 = ((bf16[32,64,512]{2,1,0:T(8,128)(2,1)}), bf16[32,64,512]{2,1,0:T(8,128)(2,1)S(1)}, u32[]{:S(2)}, u32[]{:S(2)}) async-start(bf16[32,64,512]{2,1,0:T(8,128)(2,1)} %bitcast.69), calls=%async_computation.1 | async-start | bytes 4194304 | tf_op jit(solution)/shard_map/all_to_all | solution.py:721
  211.4 46.5 %attend.1 = bf16[2,1024,128]{2,1,0:T(8,128)(2,1)} custom-call(s32[17]{0:T(128)} %compare_convert_fusion.2.side_ref, s32[17]{0:T(128)} %get-tuple-element.38.dev_ref, s32[17]{0:T(128)} %get-tuple-element.37.half_ref, s32[17]{0:T(128)} %get-tuple-element.42.diag_ref, s32[17]{0:T(128)} %get-tuple-element.41.first_ref, bf16[2,1024,128]{2,1,0:T(8,128)(2,1)} %bitcast.76, ...), custom_call_target="tpu_custom_call" | custom-call | flops 60000002048 | bytes 16777216 | tf_op jit(solution)/shard_map/attend/pallas_call | solution.py:242
  257.9 8.4 %all-to-all-start.3 = ((bf16[32,64,128]{2,1,0:T(8,128)(2,1)}), bf16[32,64,128]{2,1,0:T(8,128)(2,1)S(1)}, u32[]{:S(2)}, u32[]{:S(2)}) async-start(bf16[32,64,128]{2,1,0:T(8,128)(2,1)} %bitcast.77), calls=%async_computation.3 | async-start | bytes 1048576 | tf_op jit(solution)/shard_map/all_to_all | solution.py:722
  266.3 1.5 copy.46
  267.8 16.2 %all-to-all-done.3 = bf16[32,64,128]{2,1,0:T(8,128)(2,1)S(1)} async-done(((bf16[32,64,128]{2,1,0:T(8,128)(2,1)}), bf16[32,64,128]{2,1,0:T(8,128)(2,1)S(1)}, u32[]{:S(2)}, u32[]{:S(2)}) %all-to-all-start.3) | async-done | bytes 524320 | tf_op jit(solution)/shard_map/all_to_all | solution.py:722
  284.0 0.9 copy_bitcast_fusion.1
  (28 shorter events, 0.2 us)
Async XLA Ops:
  7.2 168.2 %copy-start = (bf16[64,4096]{1,0:T(8,128)(2,1)S(1)}, bf16[64,4096]{1,0:T(8,128)(2,1)}, u32[]{:S(2)}) copy-start(bf16[64,4096]{1,0:T(8,128)(2,1)} %param.24) | copy-start | bytes 1572868
  9.1 68.4 %copy-start.1 = (bf16[64,16384]{1,0:T(8,128)(2,1)S(1)}, bf16[64,16384]{1,0:T(8,128)(2,1)}, u32[]{:S(2)}) copy-start(bf16[64,16384]{1,0:T(8,128)(2,1)} %param.15) | copy-start | bytes 6291460
  79.1 9.5 %copy-start.6 = (f32[24,512]{1,0:T(8,128)S(1)}, f32[24,512]{1,0:T(8,128)}, u32[]{:S(2)}) copy-start(f32[24,512]{1,0:T(8,128)} %get-tuple-element.20) | copy-start | bytes 147460
  79.1 10.7 %copy-start.5 = (bf16[2,8,16,512]{3,2,1,0:T(8,128)(2,1)S(1)}, bf16[2,8,16,512]{3,2,1,0:T(8,128)(2,1)}, u32[]{:S(2)}) copy-start(bf16[2,8,16,512]{3,2,1,0:T(8,128)(2,1)} %get-tuple-element.17) | copy-start | bytes 786436
  79.1 12.5 %copy-start.7 = (s32[16]{0:T(128)S(1)}, s32[16]{0:T(128)}, u32[]{:S(2)}) copy-start(s32[16]{0:T(128)} %param.27) | copy-start | bytes 196
  79.1 97.2 %all-to-all-start = ((bf16[64,32,512]{2,0,1:T(8,128)(2,1)}), bf16[64,32,512]{2,0,1:T(8,128)(2,1)S(1)}, u32[]{:S(2)}, u32[]{:S(2)}) async-start(bf16[64,32,512]{2,0,1:T(8,128)(2,1)} %bitcast.62), calls=%async_computation | async-start | bytes 4194304 | tf_op jit(solution)/shard_map/all_to_all | solution.py:693
  87.9 123.6 %all-gather.2.cloned.1.call-start = ((), (), s32[]{:S(2)}) async-start(), calls=%async_computation.4 | async-start | bytes 8650752 | tf_op jit(solution)/shard_map/all_gather | solution.py:695
  95.8 42.8 %copy-start.3 = (bf16[256,8,32]{2,1,0:T(8,128)(2,1)S(1)}, bf16[256,8,32]{2,1,0:T(8,128)(2,1)}, u32[]{:S(2)}) copy-start(bf16[256,8,32]{2,1,0:T(8,128)(2,1)} %copy.62) | copy-start | bytes 393220
  176.3 4.3 %copy-start.2 = (bf16[64,32,512]{2,0,1:T(8,128)(2,1)}, bf16[64,32,512]{2,0,1:T(8,128)(2,1)S(1)}, u32[]{:S(2)}) copy-start(bf16[64,32,512]{2,0,1:T(8,128)(2,1)S(1)} %all-to-all-done) | copy-start | bytes 6291460
  176.3 27.0 %all-to-all-start.2 = ((bf16[64,32,128]{2,0,1:T(8,128)(2,1)}), bf16[64,32,128]{2,0,1:T(8,128)(2,1)S(1)}, u32[]{:S(2)}, u32[]{:S(2)}) async-start(bf16[64,32,128]{2,0,1:T(8,128)(2,1)} %copy_bitcast_fusion.2), calls=%async_computation.2 | async-start | bytes 1048576 | tf_op jit(solution)/shard_map/all_to_all | solution.py:694
  203.3 0.8 copy-start.4
  204.1 53.8 %all-to-all-start.1 = ((bf16[32,64,512]{2,1,0:T(8,128)(2,1)}), bf16[32,64,512]{2,1,0:T(8,128)(2,1)S(1)}, u32[]{:S(2)}, u32[]{:S(2)}) async-start(bf16[32,64,512]{2,1,0:T(8,128)(2,1)} %bitcast.69), calls=%async_computation.1 | async-start | bytes 4194304 | tf_op jit(solution)/shard_map/all_to_all | solution.py:721
  257.9 26.1 %all-to-all-start.3 = ((bf16[32,64,128]{2,1,0:T(8,128)(2,1)}), bf16[32,64,128]{2,1,0:T(8,128)(2,1)S(1)}, u32[]{:S(2)}, u32[]{:S(2)}) async-start(bf16[32,64,128]{2,1,0:T(8,128)(2,1)} %bitcast.77), calls=%async_computation.3 | async-start | bytes 1048576 | tf_op jit(solution)/shard_map/all_to_all | solution.py:722
Sparse Core Ops, SparseCore 0:
  91.2 65.3 all-gather.1

commit v2 on v1

--- a/solution.py
+++ b/solution.py
@@ -87,7 +87,7 @@
             return (hidden, run)
 
         hidden, run = lax.fori_loop(
-            0, TB, advance, (tuple(state_s[j, n] for n in range(STATE)), run_s[j]), unroll=4
+            0, TB, advance, (tuple(state_s[j, n] for n in range(STATE)), run_s[j]), unroll=8
         )
         for n in range(STATE):
             state_s[j, n] = hidden[n]
@@ -156,7 +156,7 @@
             ready_s[j, rows, :] = tree_sum(terms) + y_ref[j, rows, :]
             return carry
 
-        lax.fori_loop(0, TB, correct, 0, unroll=4)
+        lax.fori_loop(0, TB, correct, 0, unroll=8)
 
     def gate_chunk(chunk, carry):
         for j in range(TILES):
@@ -191,7 +191,7 @@
     )(y, cum, mix_out, spread, gate, rate, starts)
 
 
-QB = 256
+QB = 512
 
 
 def attention_kernel(side_ref, dev_ref, half_ref, diag_ref, first_ref, q_ref, kv_ref, o_ref, top_s, sum_s, acc_s):

time: 293 us -> 289 us (0.986)
  Pallas kernels: 202 us -> 199 us
  transfers between devices with their start and end apart: 5 -> 5, of which waited for: 1 -> 1; matrix products, arithmetic and copies ran while one was open for 6% -> 6% of each run, Pallas kernels for 48% -> 47%
where the time goes in v2:
time: 289 us; the launch traced here: 288 us
  Pallas kernels  199 us (69%)
  starting transfers between devices  28.7 us (10%)
  local copies, waits for them, and re-layouts  20.1 us (7%)
  waiting for transfers between devices  16.9 us (6%)
  between operations  14.2 us (5%)
  other arithmetic  9.13 us (3%)
    pallas_call x1, Pallas kernels, intake_call(): pl.pallas_call(intake_kernel, in_specs=[anywhere] * 5, out_specs=[anywher...  62.5 us
    pallas_call x1, Pallas kernels, attention_call(): pl.pallas_call(attention_kernel, grid_spec=pltpu.PrefetchScalarGridSpec(n...  46.6 us
    pallas_call x1, Pallas kernels, scan_call(): pl.pallas_call(scan_kernel, grid=(STEPS,), in_specs=[tokens(COLS), whole(...  41.4 us
    pallas_call x1, Pallas kernels, states_call(): pl.pallas_call(states_kernel, in_specs=[pl.BlockSpec(memory_space=pltpu.S...  27.8 us
    pallas_call x1, Pallas kernels, finish_call(): pl.pallas_call(finish_kernel, grid=(STEPS,), in_specs=[tiles, tiles, pl.B...  20.6 us
    all_to_all x1, waiting for transfers between devices, local(): lax.all_to_all(attended, ULYS, split_axis=0, concat_axis=1, tiled=True)  16.2 us
    all_to_all x1, starting transfers between devices, local(): lax.all_to_all(gate_input, PLANE, split_axis=1, concat_axis=0, tiled=True)  8.76 us
    all_to_all x1, starting transfers between devices, local(): lax.all_to_all(attended, ULYS, split_axis=0, concat_axis=1, tiled=True)  8.27 us
  transfers between devices with their start and end apart: 5, of which 1 were waited for; matrix products, arithmetic and copies ran while one was open for 6% of the time, Pallas kernels for 47%

profile of v2, /device:TPU:2, one launch (start us, length us, event | category | flops | bytes accessed | tf_op | source)
XLA Modules:
  0.0 288.2 jit_solution(9780246153283010099)
XLA Ops:
  7.2 1.0 copy.48
  8.2 0.9 copy.49
  9.1 0.8 copy.50
  9.9 0.8 copy.34
  10.7 0.8 negate_multiply_fusion
  11.5 0.1 pad.6.clone
  11.6 1.5 maximum_maximum_fusion.low_ref
  13.1 2.0 concatenate.14.params_ref
  15.0 62.5 %intake.1 = (bf16[8,4,64,512]{3,2,1,0:T(8,128)(2,1)}, bf16[8,4,64,640]{3,2,1,0:T(8,128)(2,1)}, bf16[2,8,16,512]{3,2,1,0:T(8,128)(2,1)}, bf16[8,64,256]{2,1,0:T(8...) custom-call(bf16[64,16384]{1,0:T(8,128)(2,1)} %x_ref.1, ...), custom_call_target="tpu_custom_call" | custom-call | tf_op jit(solution)/shard_map/intake/pallas_call | solution.py:507
  77.5 1.6 copy.61
  79.1 8.8 %all-to-all-start = ((bf16[64,32,512]{2,0,1:T(8,128)(2,1)}), bf16[64,32,512]{2,0,1:T(8,128)(2,1)S(1)}, u32[]{:S(2)}, u32[]{:S(2)}) async-start(bf16[64,32,512]{2,0,1:T(8,128)(2,1)} %bitcast.62), calls=%async_computation | async-start | bytes 4194304 | tf_op jit(solution)/shard_map/all_to_all | solution.py:693
  87.9 0.0 all-gather.2.cloned.1.call-start
  87.9 0.7 all-gather.2.cloned.1.call-update
  88.6 0.6 slice_bitcast_fusion.2
  89.2 0.6 fusion.16
  89.8 1.1 slice_bitcast_fusion
  90.9 0.6 slice.42.convw_ref
  91.5 0.1 reshape.123
  91.6 1.1 copy.62
  92.8 0.2 broadcast_in_dim.69
  93.0 0.8 copy.63
  93.8 0.2 add_reduce_fusion
  94.0 0.2 fusion
  94.2 1.6 convert_select_fusion.prior_ref
  95.8 41.4 %scan_chunks.1 = (f32[4,2048,128]{2,1,0:T(8,128)}, f32[4,2048,128]{2,1,0:T(8,128)}, f32[4,128,128]{2,1,0:T(8,128)}, f32[4,8,128]{2,1,0:T(8,128)}) custom-call(bf16[8,256,512]{2,1,0:T(8,128)(2,1)} %bitcast.95, f32[8,8,512]{2,1,0:T(8,128)} %convert_select_fusion.prior_ref, bf16[8,256,640]{2,1,0:T(8,128)(2,1)} %bitcast.90, bf16[2048,32]{1,0:T(8,128)(2,1)} %bitcast.71, ...), custom_call_target="tpu_custom_call" | custom-call | flops 99999997952 | bytes 16777216 | tf_op jit(solution)/shard_map/scan_chunks/pallas_call | solution.py:109
  137.2 1.0 slice.52.mix_ref
  138.2 1.5 slice.53.spread_ref
  139.7 0.6 copy.64
  140.3 0.1 dynamic_slice.7
  140.4 0.1 select_reduce_fusion.2
  140.5 0.6 pad_add_fusion.order_ref
  141.1 27.8 %chain_states.1 = f32[4,8,2,8,128]{4,3,2,1,0:T(8,128)} custom-call(s32[128]{0:T(128)} %pad_add_fusion.order_ref, f32[4,8,2,8,128]{4,3,2,1,0:T(8,128)} %bitcast.84, f32[4,8,128]{2,1,0:T(8,128)} %get-tuple-element.25.sum_ref, f32[4,2,8,128]{3,2,1,0:T(8,128)} %bitcast.88), custom_call_target="tpu_custom_call" | custom-call | tf_op jit(solution)/shard_map/chain_states/pallas_call | solution.py:629
  168.8 0.6 fusion.17
  169.4 0.6 compare_select_fusion.9
  170.1 1.2 compare_convert_fusion.2.side_ref
  171.3 1.8 compare_convert_fusion
  173.1 0.1 select_reduce_fusion
  173.2 0.6 and_select_fusion
  173.8 1.0 copy_bitcast_fusion.2
  174.8 4.5 %all-to-all-start.2 = ((bf16[64,32,128]{2,0,1:T(8,128)(2,1)}), bf16[64,32,128]{2,0,1:T(8,128)(2,1)S(1)}, u32[]{:S(2)}, u32[]{:S(2)}) async-start(bf16[64,32,128]{2,0,1:T(8,128)(2,1)} %copy_bitcast_fusion.2), calls=%async_computation.2 | async-start | bytes 1048576 | tf_op jit(solution)/shard_map/all_to_all | solution.py:694
  179.3 20.6 %finish_chunks.1 = bf16[8,256,512]{2,1,0:T(8,128)(2,1)} custom-call(f32[4,2048,128]{2,1,0:T(8,128)} %get-tuple-element.21.y_ref, f32[4,2048,128]{2,1,0:T(8,128)} %get-tuple-element.22.cum_ref, bf16[2048,16]{1,0:T(8,128)(2,1)} %slice.52.mix_ref, bf16[16,2048]{1,0:T(8,128)(2,1)} %slice.53.spread_ref, bf16[8,256,512]{2,1,0:T(8,128)(2,1)} %bitcast.68, ...), custom_call_target="tpu_custom_call" | custom-call | flops 49999998976 | bytes 16777216 | tf_op jit(solution)/shard_map/finish_chunks/pallas_call | solution.py:178
  199.9 0.8 copy-done.4
  200.7 7.2 %all-to-all-start.1 = ((bf16[32,64,512]{2,1,0:T(8,128)(2,1)}), bf16[32,64,512]{2,1,0:T(8,128)(2,1)S(1)}, u32[]{:S(2)}, u32[]{:S(2)}) async-start(bf16[32,64,512]{2,1,0:T(8,128)(2,1)} %bitcast.69), calls=%async_computation.1 | async-start | bytes 4194304 | tf_op jit(solution)/shard_map/all_to_all | solution.py:721
  207.9 46.6 %attend.1 = bf16[2,1024,128]{2,1,0:T(8,128)(2,1)} custom-call(s32[17]{0:T(128)} %compare_convert_fusion.2.side_ref, s32[17]{0:T(128)} %get-tuple-element.38.dev_ref, s32[17]{0:T(128)} %get-tuple-element.37.half_ref, s32[17]{0:T(128)} %get-tuple-element.42.diag_ref, s32[17]{0:T(128)} %get-tuple-element.41.first_ref, bf16[2,1024,128]{2,1,0:T(8,128)(2,1)} %bitcast.76, ...), custom_call_target="tpu_custom_call" | custom-call | flops 60000002048 | bytes 16777216 | tf_op jit(solution)/shard_map/attend/pallas_call | solution.py:242
  254.5 8.3 %all-to-all-start.3 = ((bf16[32,64,128]{2,1,0:T(8,128)(2,1)}), bf16[32,64,128]{2,1,0:T(8,128)(2,1)S(1)}, u32[]{:S(2)}, u32[]{:S(2)}) async-start(bf16[32,64,128]{2,1,0:T(8,128)(2,1)} %bitcast.77), calls=%async_computation.3 | async-start | bytes 1048576 | tf_op jit(solution)/shard_map/all_to_all | solution.py:722
  262.8 1.5 copy.46
  264.3 16.2 %all-to-all-done.3 = bf16[32,64,128]{2,1,0:T(8,128)(2,1)S(1)} async-done(((bf16[32,64,128]{2,1,0:T(8,128)(2,1)}), bf16[32,64,128]{2,1,0:T(8,128)(2,1)S(1)}, u32[]{:S(2)}, u32[]{:S(2)}) %all-to-all-start.3) | async-done | bytes 524320 | tf_op jit(solution)/shard_map/all_to_all | solution.py:722
  280.5 0.9 copy_bitcast_fusion.1
  (28 shorter events, 0.2 us)
Async XLA Ops:
  7.2 166.6 %copy-start = (bf16[64,4096]{1,0:T(8,128)(2,1)S(1)}, bf16[64,4096]{1,0:T(8,128)(2,1)}, u32[]{:S(2)}) copy-start(bf16[64,4096]{1,0:T(8,128)(2,1)} %param.24) | copy-start | bytes 1572868
  9.1 68.4 %copy-start.1 = (bf16[64,16384]{1,0:T(8,128)(2,1)S(1)}, bf16[64,16384]{1,0:T(8,128)(2,1)}, u32[]{:S(2)}) copy-start(bf16[64,16384]{1,0:T(8,128)(2,1)} %param.15) | copy-start | bytes 6291460
  79.1 9.5 %copy-start.6 = (f32[24,512]{1,0:T(8,128)S(1)}, f32[24,512]{1,0:T(8,128)}, u32[]{:S(2)}) copy-start(f32[24,512]{1,0:T(8,128)} %get-tuple-element.20) | copy-start | bytes 147460
  79.1 10.7 %copy-start.5 = (bf16[2,8,16,512]{3,2,1,0:T(8,128)(2,1)S(1)}, bf16[2,8,16,512]{3,2,1,0:T(8,128)(2,1)}, u32[]{:S(2)}) copy-start(bf16[2,8,16,512]{3,2,1,0:T(8,128)(2,1)} %get-tuple-element.17) | copy-start | bytes 786436
  79.1 12.5 %copy-start.7 = (s32[16]{0:T(128)S(1)}, s32[16]{0:T(128)}, u32[]{:S(2)}) copy-start(s32[16]{0:T(128)} %param.27) | copy-start | bytes 196
  79.1 95.7 %all-to-all-start = ((bf16[64,32,512]{2,0,1:T(8,128)(2,1)}), bf16[64,32,512]{2,0,1:T(8,128)(2,1)S(1)}, u32[]{:S(2)}, u32[]{:S(2)}) async-start(bf16[64,32,512]{2,0,1:T(8,128)(2,1)} %bitcast.62), calls=%async_computation | async-start | bytes 4194304 | tf_op jit(solution)/shard_map/all_to_all | solution.py:693
  87.9 120.0 %all-gather.2.cloned.1.call-start = ((), (), s32[]{:S(2)}) async-start(), calls=%async_computation.4 | async-start | bytes 8650752 | tf_op jit(solution)/shard_map/all_gather | solution.py:695
  95.8 41.4 %copy-start.3 = (bf16[256,8,32]{2,1,0:T(8,128)(2,1)S(1)}, bf16[256,8,32]{2,1,0:T(8,128)(2,1)}, u32[]{:S(2)}) copy-start(bf16[256,8,32]{2,1,0:T(8,128)(2,1)} %copy.62) | copy-start | bytes 393220
  174.8 4.5 %copy-start.2 = (bf16[64,32,512]{2,0,1:T(8,128)(2,1)}, bf16[64,32,512]{2,0,1:T(8,128)(2,1)S(1)}, u32[]{:S(2)}) copy-start(bf16[64,32,512]{2,0,1:T(8,128)(2,1)S(1)} %all-to-all-done) | copy-start | bytes 6291460
  174.8 25.1 %all-to-all-start.2 = ((bf16[64,32,128]{2,0,1:T(8,128)(2,1)}), bf16[64,32,128]{2,0,1:T(8,128)(2,1)S(1)}, u32[]{:S(2)}, u32[]{:S(2)}) async-start(bf16[64,32,128]{2,0,1:T(8,128)(2,1)} %copy_bitcast_fusion.2), calls=%async_computation.2 | async-start | bytes 1048576 | tf_op jit(solution)/shard_map/all_to_all | solution.py:694
  199.9 0.8 copy-start.4
  200.7 53.8 %all-to-all-start.1 = ((bf16[32,64,512]{2,1,0:T(8,128)(2,1)}), bf16[32,64,512]{2,1,0:T(8,128)(2,1)S(1)}, u32[]{:S(2)}, u32[]{:S(2)}) async-start(bf16[32,64,512]{2,1,0:T(8,128)(2,1)} %bitcast.69), calls=%async_computation.1 | async-start | bytes 4194304 | tf_op jit(solution)/shard_map/all_to_all | solution.py:721
  254.5 26.0 %all-to-all-start.3 = ((bf16[32,64,128]{2,1,0:T(8,128)(2,1)}), bf16[32,64,128]{2,1,0:T(8,128)(2,1)S(1)}, u32[]{:S(2)}, u32[]{:S(2)}) async-start(bf16[32,64,128]{2,1,0:T(8,128)(2,1)} %bitcast.77), calls=%async_computation.3 | async-start | bytes 1048576 | tf_op jit(solution)/shard_map/all_to_all | solution.py:722
Sparse Core Ops, SparseCore 0:
  91.2 65.3 all-gather.1

commit v3 on v2

--- a/solution.py
+++ b/solution.py
@@ -31,7 +31,7 @@
 def scan_kernel(
     x_ref, prior_ref, low_ref, mix_ref, spread_ref, w_ref, convw_ref, convb_ref, bias_ref, rate_ref, skip_ref,
     y_ref, cum_ref, end_ref, sum_ref,
-    delta_s, dx_s, direct_s, splat_s, tail_s, state_s, run_s,
+    delta_s, dx_s, direct_s, splat_s, tail_s, state_s, run_s, raw_s,
 ):
     step = pl.program_id(0)
 
@@ -42,6 +42,10 @@
         run_s[...] = jnp.zeros_like(run_s)
 
     splat_s[...] = jnp.dot(mix_ref[...], spread_ref[...], preferred_element_type=jnp.float32)
+
+    raw_s[...] = jnp.dot(
+        low_ref[...].reshape(CHUNKS * TB, 512), w_ref[...], preferred_element_type=jnp.float32
+    )
 
     def prepare(chunk, carry):
         x = x_ref[chunk].astype(jnp.float32)
@@ -51,7 +55,7 @@
             mixed = mixed + convw_ref[k : k + 1, :] * padded[8 - (CONV - 1) + k : 8 - (CONV - 1) + k + TB]
         tail_s[chunk] = x[TB - 8 :]
         driven = mixed * jax.nn.sigmoid(mixed)
-        raw = jnp.dot(low_ref[chunk], w_ref[...], preferred_element_type=jnp.float32) + bias_ref[...]
+        raw = raw_s[pl.ds(pl.multiple_of(chunk * TB, TB), TB), :] + bias_ref[...]
         delta = jnp.maximum(raw, 0.0) + jnp.log1p(jnp.exp(-jnp.abs(raw)))
         dx = delta * driven
         direct = skip_ref[...] * driven
@@ -130,7 +134,7 @@
             pltpu.VMEM((TILES, rows, 128), f32), pltpu.VMEM((TILES, rows, 128), f32),
             pltpu.VMEM((TILES, rows, 128), f32), pltpu.VMEM((rows, 2 * STATE * 128), f32),
             pltpu.VMEM((CHUNKS, 8, COLS), f32), pltpu.VMEM((TILES, STATE, CHUNKS, 128), f32),
-            pltpu.VMEM((TILES, CHUNKS, 128), f32),
+            pltpu.VMEM((TILES, CHUNKS, 128), f32), pltpu.VMEM((rows, COLS), f32),
         ],
         compiler_params=pltpu.CompilerParams(vmem_limit_bytes=VMEM_LIMIT),
         cost_estimate=pl.CostEstimate(flops=100_000_000_000, bytes_accessed=16 * 2**20, transcendentals=0),

time: 289 us -> 281 us (0.972)
  Pallas kernels: 199 us -> 191 us
    pallas_call x1, Pallas kernels: 41.4 us -> 32.9 us  [scan_call(): pl.pallas_call(scan_kernel, grid=(STEPS,), in_specs=[tokens(COLS), whole(...]
  transfers between devices with their start and end apart: 5 -> 5, of which waited for: 1 -> 1; matrix products, arithmetic and copies ran while one was open for 6% -> 7% of each run, Pallas kernels for 47% -> 46%
where the time goes in v3:
time: 281 us; the launch traced here: 280 us
  Pallas kernels  191 us (68%)
  starting transfers between devices  28.8 us (10%)
  local copies, waits for them, and re-layouts  20.1 us (7%)
  waiting for transfers between devices  16.9 us (6%)
  between operations  14.2 us (5%)
  other arithmetic  9.13 us (3%)
    pallas_call x1, Pallas kernels, intake_call(): pl.pallas_call(intake_kernel, in_specs=[anywhere] * 5, out_specs=[anywher...  62.5 us
    pallas_call x1, Pallas kernels, attention_call(): pl.pallas_call(attention_kernel, grid_spec=pltpu.PrefetchScalarGridSpec(n...  46.6 us
    pallas_call x1, Pallas kernels, scan_call(): pl.pallas_call(scan_kernel, grid=(STEPS,), in_specs=[tokens(COLS), whole(...  32.9 us
    pallas_call x1, Pallas kernels, states_call(): pl.pallas_call(states_kernel, in_specs=[pl.BlockSpec(memory_space=pltpu.S...  28.1 us
    pallas_call x1, Pallas kernels, finish_call(): pl.pallas_call(finish_kernel, grid=(STEPS,), in_specs=[tiles, tiles, pl.B...  20.6 us
    all_to_all x1, waiting for transfers between devices, local(): lax.all_to_all(attended, ULYS, split_axis=0, concat_axis=1, tiled=True)  16.2 us
    all_to_all x1, starting transfers between devices, local(): lax.all_to_all(gate_input, PLANE, split_axis=1, concat_axis=0, tiled=True)  8.76 us
    all_to_all x1, starting transfers between devices, local(): lax.all_to_all(attended, ULYS, split_axis=0, concat_axis=1, tiled=True)  8.27 us
  transfers between devices with their start and end apart: 5, of which 1 were waited for; matrix products, arithmetic and copies ran while one was open for 7% of the time, Pallas kernels for 46%

profile of v3, /device:TPU:2, one launch (start us, length us, event | category | flops | bytes accessed | tf_op | source)
XLA Modules:
  0.0 280.1 jit_solution(14093167004971979438)
XLA Ops:
  7.2 1.0 copy.48
  8.2 0.9 copy.49
  9.1 0.8 copy.50
  9.9 0.8 copy.34
  10.7 0.8 negate_multiply_fusion
  11.5 0.1 pad.6.clone
  11.6 1.5 maximum_maximum_fusion.low_ref
  13.1 2.0 concatenate.14.params_ref
  15.0 62.5 %intake.1 = (bf16[8,4,64,512]{3,2,1,0:T(8,128)(2,1)}, bf16[8,4,64,640]{3,2,1,0:T(8,128)(2,1)}, bf16[2,8,16,512]{3,2,1,0:T(8,128)(2,1)}, bf16[8,64,256]{2,1,0:T(8...) custom-call(bf16[64,16384]{1,0:T(8,128)(2,1)} %x_ref.1, ...), custom_call_target="tpu_custom_call" | custom-call | tf_op jit(solution)/shard_map/intake/pallas_call | solution.py:511
  77.5 1.6 copy.61
  79.1 8.8 %all-to-all-start = ((bf16[64,32,512]{2,0,1:T(8,128)(2,1)}), bf16[64,32,512]{2,0,1:T(8,128)(2,1)S(1)}, u32[]{:S(2)}, u32[]{:S(2)}) async-start(bf16[64,32,512]{2,0,1:T(8,128)(2,1)} %bitcast.62), calls=%async_computation | async-start | bytes 4194304 | tf_op jit(solution)/shard_map/all_to_all | solution.py:697
  87.9 0.0 all-gather.2.cloned.1.call-start
  87.9 0.7 all-gather.2.cloned.1.call-update
  88.6 0.6 slice_bitcast_fusion.2
  89.2 0.6 fusion.16
  89.8 1.1 slice_bitcast_fusion
  90.9 0.6 slice.42.convw_ref
  91.5 0.1 reshape.123
  91.6 1.1 copy.62
  92.8 0.2 broadcast_in_dim.69
  93.0 0.8 copy.63
  93.8 0.2 add_reduce_fusion
  94.0 0.2 fusion
  94.2 1.6 convert_select_fusion.prior_ref
  95.8 32.9 %scan_chunks.1 = (f32[4,2048,128]{2,1,0:T(8,128)}, f32[4,2048,128]{2,1,0:T(8,128)}, f32[4,128,128]{2,1,0:T(8,128)}, f32[4,8,128]{2,1,0:T(8,128)}) custom-call(bf16[8,256,512]{2,1,0:T(8,128)(2,1)} %bitcast.95, f32[8,8,512]{2,1,0:T(8,128)} %convert_select_fusion.prior_ref, bf16[8,256,640]{2,1,0:T(8,128)(2,1)} %bitcast.90, bf16[2048,32]{1,0:T(8,128)(2,1)} %bitcast.71, ...), custom_call_target="tpu_custom_call" | custom-call | flops 99999997952 | bytes 16777216 | tf_op jit(solution)/shard_map/scan_chunks/pallas_call | solution.py:113
  128.7 1.0 slice.52.mix_ref
  129.7 1.5 slice.53.spread_ref
  131.2 0.6 copy.64
  131.8 0.1 dynamic_slice.7
  131.9 0.1 select_reduce_fusion.2
  132.0 0.6 pad_add_fusion.order_ref
  132.6 28.1 %chain_states.1 = f32[4,8,2,8,128]{4,3,2,1,0:T(8,128)} custom-call(s32[128]{0:T(128)} %pad_add_fusion.order_ref, f32[4,8,2,8,128]{4,3,2,1,0:T(8,128)} %bitcast.84, f32[4,8,128]{2,1,0:T(8,128)} %get-tuple-element.25.sum_ref, f32[4,2,8,128]{3,2,1,0:T(8,128)} %bitcast.88), custom_call_target="tpu_custom_call" | custom-call | tf_op jit(solution)/shard_map/chain_states/pallas_call | solution.py:633
  160.7 0.6 fusion.17
  161.3 0.6 compare_select_fusion.9
  161.9 1.2 compare_convert_fusion.2.side_ref
  163.1 1.8 compare_convert_fusion
  165.0 0.1 select_reduce_fusion
  165.1 0.6 and_select_fusion
  165.6 1.0 copy_bitcast_fusion.2
  166.6 4.5 %all-to-all-start.2 = ((bf16[64,32,128]{2,0,1:T(8,128)(2,1)}), bf16[64,32,128]{2,0,1:T(8,128)(2,1)S(1)}, u32[]{:S(2)}, u32[]{:S(2)}) async-start(bf16[64,32,128]{2,0,1:T(8,128)(2,1)} %copy_bitcast_fusion.2), calls=%async_computation.2 | async-start | bytes 1048576 | tf_op jit(solution)/shard_map/all_to_all | solution.py:698
  171.2 20.6 %finish_chunks.1 = bf16[8,256,512]{2,1,0:T(8,128)(2,1)} custom-call(f32[4,2048,128]{2,1,0:T(8,128)} %get-tuple-element.21.y_ref, f32[4,2048,128]{2,1,0:T(8,128)} %get-tuple-element.22.cum_ref, bf16[2048,16]{1,0:T(8,128)(2,1)} %slice.52.mix_ref, bf16[16,2048]{1,0:T(8,128)(2,1)} %slice.53.spread_ref, bf16[8,256,512]{2,1,0:T(8,128)(2,1)} %bitcast.68, ...), custom_call_target="tpu_custom_call" | custom-call | flops 49999998976 | bytes 16777216 | tf_op jit(solution)/shard_map/finish_chunks/pallas_call | solution.py:182
  191.8 0.8 copy-done.4
  192.6 7.2 %all-to-all-start.1 = ((bf16[32,64,512]{2,1,0:T(8,128)(2,1)}), bf16[32,64,512]{2,1,0:T(8,128)(2,1)S(1)}, u32[]{:S(2)}, u32[]{:S(2)}) async-start(bf16[32,64,512]{2,1,0:T(8,128)(2,1)} %bitcast.69), calls=%async_computation.1 | async-start | bytes 4194304 | tf_op jit(solution)/shard_map/all_to_all | solution.py:725
  199.8 46.6 %attend.1 = bf16[2,1024,128]{2,1,0:T(8,128)(2,1)} custom-call(s32[17]{0:T(128)} %compare_convert_fusion.2.side_ref, s32[17]{0:T(128)} %get-tuple-element.38.dev_ref, s32[17]{0:T(128)} %get-tuple-element.37.half_ref, s32[17]{0:T(128)} %get-tuple-element.42.diag_ref, s32[17]{0:T(128)} %get-tuple-element.41.first_ref, bf16[2,1024,128]{2,1,0:T(8,128)(2,1)} %bitcast.76, ...), custom_call_target="tpu_custom_call" | custom-call | flops 60000002048 | bytes 16777216 | tf_op jit(solution)/shard_map/attend/pallas_call | solution.py:246
  246.4 8.3 %all-to-all-start.3 = ((bf16[32,64,128]{2,1,0:T(8,128)(2,1)}), bf16[32,64,128]{2,1,0:T(8,128)(2,1)S(1)}, u32[]{:S(2)}, u32[]{:S(2)}) async-start(bf16[32,64,128]{2,1,0:T(8,128)(2,1)} %bitcast.77), calls=%async_computation.3 | async-start | bytes 1048576 | tf_op jit(solution)/shard_map/all_to_all | solution.py:726
  254.7 1.5 copy.46
  256.2 16.2 %all-to-all-done.3 = bf16[32,64,128]{2,1,0:T(8,128)(2,1)S(1)} async-done(((bf16[32,64,128]{2,1,0:T(8,128)(2,1)}), bf16[32,64,128]{2,1,0:T(8,128)(2,1)S(1)}, u32[]{:S(2)}, u32[]{:S(2)}) %all-to-all-start.3) | async-done | bytes 524320 | tf_op jit(solution)/shard_map/all_to_all | solution.py:726
  272.4 0.9 copy_bitcast_fusion.1
  (28 shorter events, 0.2 us)
Async XLA Ops:
  7.2 158.5 %copy-start = (bf16[64,4096]{1,0:T(8,128)(2,1)S(1)}, bf16[64,4096]{1,0:T(8,128)(2,1)}, u32[]{:S(2)}) copy-start(bf16[64,4096]{1,0:T(8,128)(2,1)} %param.24) | copy-start | bytes 1572868
  9.1 68.4 %copy-start.1 = (bf16[64,16384]{1,0:T(8,128)(2,1)S(1)}, bf16[64,16384]{1,0:T(8,128)(2,1)}, u32[]{:S(2)}) copy-start(bf16[64,16384]{1,0:T(8,128)(2,1)} %param.15) | copy-start | bytes 6291460
  79.1 9.5 %copy-start.6 = (f32[24,512]{1,0:T(8,128)S(1)}, f32[24,512]{1,0:T(8,128)}, u32[]{:S(2)}) copy-start(f32[24,512]{1,0:T(8,128)} %get-tuple-element.20) | copy-start | bytes 147460
  79.1 10.7 %copy-start.5 = (bf16[2,8,16,512]{3,2,1,0:T(8,128)(2,1)S(1)}, bf16[2,8,16,512]{3,2,1,0:T(8,128)(2,1)}, u32[]{:S(2)}) copy-start(bf16[2,8,16,512]{3,2,1,0:T(8,128)(2,1)} %get-tuple-element.17) | copy-start | bytes 786436
  79.1 12.5 %copy-start.7 = (s32[16]{0:T(128)S(1)}, s32[16]{0:T(128)}, u32[]{:S(2)}) copy-start(s32[16]{0:T(128)} %param.27) | copy-start | bytes 196
  79.1 87.5 %all-to-all-start = ((bf16[64,32,512]{2,0,1:T(8,128)(2,1)}), bf16[64,32,512]{2,0,1:T(8,128)(2,1)S(1)}, u32[]{:S(2)}, u32[]{:S(2)}) async-start(bf16[64,32,512]{2,0,1:T(8,128)(2,1)} %bitcast.62), calls=%async_computation | async-start | bytes 4194304 | tf_op jit(solution)/shard_map/all_to_all | solution.py:697
  87.9 112.0 %all-gather.2.cloned.1.call-start = ((), (), s32[]{:S(2)}) async-start(), calls=%async_computation.4 | async-start | bytes 8650752 | tf_op jit(solution)/shard_map/all_gather | solution.py:699
  95.8 32.9 %copy-start.3 = (bf16[256,8,32]{2,1,0:T(8,128)(2,1)S(1)}, bf16[256,8,32]{2,1,0:T(8,128)(2,1)}, u32[]{:S(2)}) copy-start(bf16[256,8,32]{2,1,0:T(8,128)(2,1)} %copy.62) | copy-start | bytes 393220
  166.6 4.5 %copy-start.2 = (bf16[64,32,512]{2,0,1:T(8,128)(2,1)}, bf16[64,32,512]{2,0,1:T(8,128)(2,1)S(1)}, u32[]{:S(2)}) copy-start(bf16[64,32,512]{2,0,1:T(8,128)(2,1)S(1)} %all-to-all-done) | copy-start | bytes 6291460
  166.6 25.2 %all-to-all-start.2 = ((bf16[64,32,128]{2,0,1:T(8,128)(2,1)}), bf16[64,32,128]{2,0,1:T(8,128)(2,1)S(1)}, u32[]{:S(2)}, u32[]{:S(2)}) async-start(bf16[64,32,128]{2,0,1:T(8,128)(2,1)} %copy_bitcast_fusion.2), calls=%async_computation.2 | async-start | bytes 1048576 | tf_op jit(solution)/shard_map/all_to_all | solution.py:698
  191.8 0.8 copy-start.4
  192.6 53.9 %all-to-all-start.1 = ((bf16[32,64,512]{2,1,0:T(8,128)(2,1)}), bf16[32,64,512]{2,1,0:T(8,128)(2,1)S(1)}, u32[]{:S(2)}, u32[]{:S(2)}) async-start(bf16[32,64,512]{2,1,0:T(8,128)(2,1)} %bitcast.69), calls=%async_computation.1 | async-start | bytes 4194304 | tf_op jit(solution)/shard_map/all_to_all | solution.py:725
  246.4 26.0 %all-to-all-start.3 = ((bf16[32,64,128]{2,1,0:T(8,128)(2,1)}), bf16[32,64,128]{2,1,0:T(8,128)(2,1)S(1)}, u32[]{:S(2)}, u32[]{:S(2)}) async-start(bf16[32,64,128]{2,1,0:T(8,128)(2,1)} %bitcast.77), calls=%async_computation.3 | async-start | bytes 1048576 | tf_op jit(solution)/shard_map/all_to_all | solution.py:726
Sparse Core Ops, SparseCore 0:
  91.2 65.3 all-gather.1
